TPU v7x, 128 devices: a whole 4x4x4 slice. The times are simulated.
128 devices in a mesh: prow: 8 (over z, y_hi), pcol: 16 (over x, y_lo, core).
Axes of the slice: x: 4, y: 4 (y_hi: 2, y_lo: 2; y = y_hi * 2 + y_lo), z: 4, core: 2. Of those that a mesh axis runs over, the one named last changes fastest.
Arguments:
- pair_act: float32 [512, 512, 128], P('prow', 'pcol'), may hold values from -6 to 6
- token_mask: int32 [512], replicated, may hold values from 0 to 1
- w_proj: bfloat16 [4, 128, 128], replicated, may hold values from -0.5 to 0.5
- w_bias: bfloat16 [128, 4], replicated, may hold values from -30 to 30
- w_out: bfloat16 [128, 128], replicated, may hold values from -0.5 to 0.5
- cotangent: bfloat16 [512, 512, 128], P('prow', 'pcol'), may hold values from -6 to 6
Outputs:
- update: float32 [512, 512, 128], P('prow', 'pcol')
- d_pair: float32 [512, 512, 128], P('prow', 'pcol')
All inputs are finite; a program needn't handle non-finite values.
Results may differ from a plain program's by a relative error of at most 0.005.
The roundings to bfloat16 on the way count: a program that leaves them out, or rounds other values in their place, can miss the bound.
Values may be sent and summed in bfloat16 or wider, within the bound.
No kernel may reach another device: no remote copies, remote signals or barrier semaphores. Data moves between devices by JAX's collectives and lax.ppermute only.
A program may use at most 192 MiB of HBM per device.

v0:
```python
import functools
import math

import jax
import jax.numpy as jnp
from jax import lax
from jax.experimental import pallas as pl
from jax.experimental.pallas import tpu as pltpu
from jax.sharding import Mesh, PartitionSpec as P

norm_eps = 1e-05
masked_score = -1000000000.0
code_top = 32000.0
RA = 2
RB = 2
GP = 4
GM = 4
GF = 4
F32 = jnp.float32
BF16 = jnp.bfloat16
CHIP = ("x", "yl")
CELL = ("x", "yl", "c")
NEAR = ("yh", "x", "yl", "c")


def dot(left, right):
    return lax.dot_general(left, right, (((1,), (0,)), ((), ())), preferred_element_type=F32)


def dot_t(left, right):
    return lax.dot_general(left, right, (((1,), (1,)), ((), ())), preferred_element_type=F32)


def dot_exact(left, right):
    high = left.astype(BF16)
    low = (left - high.astype(F32)).astype(BF16)
    return dot(high, right) + dot(low, right)


def lanes(shape):
    return lax.broadcasted_iota(jnp.int32, shape, len(shape) - 1)


def normalize(pair_act):
    average = jnp.mean(pair_act, axis=-1, keepdims=True)
    centred = pair_act - average
    spread = jnp.mean(centred * centred, axis=-1, keepdims=True)
    inverse = lax.rsqrt(spread + norm_eps)
    return (centred * inverse, inverse)


def prepare_kernel(pair_ref, cot_ref, live_ref, w_spread_ref, sent_ref, bias_ref):
    rows, cells, width = pair_ref.shape
    lanes_of_head = w_spread_ref.shape[1] // 4
    step = pl.program_id(0)
    normed_b = normalize(pair_ref[...])[0].astype(BF16)
    sent_ref[..., :width] = normed_b.reshape(sent_ref.shape[:-1] + (width,))
    sent_ref[..., width:] = cot_ref[...].reshape(sent_ref.shape[:-1] + (width,))
    spread = dot(normed_b.reshape(rows * cells, width), w_spread_ref[...]).reshape(rows, cells, -1)
    lane = lanes(spread.shape[1:])
    for c in range(2):
        half = slice(c * width, (c + 1) * width)
        total = bias_ref[c]
        for r in range(rows):
            here = lax.rem(lane[:, half], lanes_of_head) == step * rows + r
            total = jnp.where(here, jnp.where(live_ref[...] > 0, spread[r, :, half], masked_score), total)
        bias_ref[c] = total

    @pl.when(step == pl.num_programs(0) - 1)
    def _():
        for n in range(2, bias_ref.shape[0]):
            bias_ref[n] = bias_ref[n % 2]


def after_kernel(*refs):
    pass


def turn_kernel(where_ref, came_ref, out_ref):
    rows = out_ref.shape[1] // 2
    for t in range(2):
        block = came_ref[lax.rem(where_ref[2] + t, 2)].T
        for h in range(out_ref.shape[0]):
            out_ref[h, t * rows : (t + 1) * rows] = block[h * rows : (h + 1) * rows]


def turn_back_kernel(where_ref, *refs):
    here_ref, *came_refs, out_ref = refs
    total = here_ref[...]
    n_tokens = total.shape[-1]
    for ref in came_refs:
        quarters = ref[..., n_tokens:].astype(jnp.int32).astype(F32)
        total = total + decode(ref[..., :n_tokens], jnp.max(quarters, axis=-1, keepdims=True))
    rows = total.shape[1] // 2
    for t in range(2):
        both = total[:, t * rows : (t + 1) * rows].reshape(total.shape[0] * rows, -1)
        out_ref[lax.rem(where_ref[2] + t, 2)] = both.T.reshape(out_ref.shape[1:])


def weights_kernel(half, where_ref, w_proj_ref, w_out_ref, w_in_ref, w_back_ref, w_dm_ref):
    first = where_ref[0] == 0

    def mine(w):
        w = w.astype(F32)
        return jnp.where(first, w[:, :half], w[:, half:])

    w_in = jnp.concatenate([mine(w_proj_ref[n]) for n in (0, 3, 1, 2)], axis=1)
    w_in_ref[...] = w_in.astype(BF16)
    w_back_ref[...] = w_in.T.astype(BF16)
    w_dm = mine(w_out_ref[...].astype(F32).T)
    w_dm_ref[...] = jnp.concatenate([jnp.zeros_like(w_dm), w_dm], axis=1).astype(BF16)


def project(half, scale_q, first, own, other, live, w_in, w_dm):
    chips, cells, wide = own.shape
    width = wide // 2
    tokens = jnp.stack([jnp.where(first, own, other), jnp.where(first, other, own)], axis=1)
    tokens = tokens.reshape(chips * 2 * cells, wide)
    normed_b, cot = tokens[:, :width], tokens[:, width:]
    both = dot(normed_b, w_in)
    q_gate, key_value = both[:, : 2 * half], both[:, 2 * half :]
    low = lanes(q_gate.shape) < half
    gate = jax.nn.sigmoid(q_gate)
    d_att = dot(cot, w_dm) * gate
    qd = jnp.where(low, q_gate * scale_q, d_att).astype(BF16)
    kv = key_value.astype(BF16)
    kvm = jnp.where(low & (live == 0), 0.0, kv.astype(F32)).astype(BF16)
    return qd, kv, kvm, jnp.where(low, pltpu.roll(gate, half, 1), d_att)


def encode(values):
    most = jnp.maximum(jnp.max(jnp.abs(values), axis=-1, keepdims=True), 1e-30)
    quarters = jnp.floor(jnp.log(most) * (4.0 / math.log(2.0))) + 2.0
    codes = jnp.floor(values * (code_top * jnp.exp2(quarters * -0.25)) + 0.5)
    return codes.astype(jnp.int32).astype(jnp.int16), quarters


def decode(codes, quarters):
    return codes.astype(jnp.int32).astype(F32) * (jnp.exp2(quarters * 0.25) * (1.0 / code_top))


def hand_over(dbias_refs, out_refs):
    @pl.when(pl.program_id(0) == pl.num_programs(0) - 1)
    def _():
        for ref, out_ref in zip(dbias_refs, out_refs):
            n_tokens = ref.shape[-1]
            codes, quarters = encode(ref[...])
            out_ref[..., :n_tokens] = codes
            quarters = jnp.broadcast_to(quarters, codes.shape[:-1] + (out_ref.shape[-1] - n_tokens,))
            out_ref[..., n_tokens:] = quarters.astype(jnp.int32).astype(jnp.int16)


def attend(half, head_dim, scale_q, rows, bias_refs, dbias_refs):
    heads = range(half // head_dim)
    each = [(r, h) for r in range(len(rows)) for h in heads]
    block = bias_refs[0].shape[1]
    qds, ges, kvs, kvms = zip(*rows)
    lane = lanes(qds[0].shape)
    zero = jnp.zeros_like(qds[0])

    def own(h, base):
        return (lane >= base + h * head_dim) & (lane < base + (h + 1) * head_dim)

    scores = {(r, h): dot_t(jnp.where(own(h, 0), qds[r], zero), kvms[r]) for r, h in each}
    d_probs = {(r, h): dot_t(jnp.where(own(h, half), qds[r], zero), kvms[r]) for r, h in each}
    qd_t = [qd.astype(F32).T.astype(BF16) for qd in qds]
    attention, low = {}, {}
    for r, h in each:
        biased = [scores[r, h][n * block : (n + 1) * block] + ref[h] for n, ref in enumerate(bias_refs)]
        biased = jnp.concatenate(biased, axis=0)
        weights = jnp.exp(biased - jnp.max(biased, axis=-1, keepdims=True))
        attention[r, h] = weights * (1.0 / jnp.sum(weights, axis=-1, keepdims=True))
        low[r, h] = attention[r, h].astype(BF16)
    attended = [jnp.zeros(lane.shape, F32) for _ in rows]
    for r, h in each:
        attended[r] = jnp.where(own(h, half), dot(low[r, h], kvs[r]), attended[r])
    edge = [ge * att for ge, att in zip(ges, attended)]
    d_low = {}
    for h in heads:
        total = None
        for r in range(len(rows)):
            delta = jnp.sum(jnp.where(own(h, half), edge[r], 0.0), axis=-1, keepdims=True)
            d_scores = attention[r, h] * (d_probs[r, h] - delta)
            total = d_scores if total is None else total + d_scores
            d_low[r, h] = d_scores.astype(BF16)
        for n, ref in enumerate(dbias_refs):
            ref[h] += total[n * block : (n + 1) * block]
    results = []
    for r in range(len(rows)):
        gate = pltpu.roll(ges[r], half, 1)
        dqg = edge[r] * (1.0 - gate)
        for h in heads:
            dqg = jnp.where(own(h, 0), dot(d_low[r, h], kvs[r]) * scale_q, dqg)
        d_key = [dot(qd_t[r][h * head_dim : (h + 1) * head_dim], d_low[r, h]) for h in heads]
        d_value = [dot(qd_t[r][half + h * head_dim : half + (h + 1) * head_dim], low[r, h]) for h in heads]
        mixed = jnp.where(lane >= half, gate * attended[r], 0.0)
        results.append((dqg, mixed, jnp.concatenate(d_key + d_value, axis=0)))
    return results


def clear(refs):
    @pl.when(pl.program_id(0) == 0)
    def _():
        for ref in refs:
            ref[...] = jnp.zeros_like(ref)


def places(where_ref, steps, n_z, rows_j):
    at = [lax.rem(where_ref[1] + s, n_z) * 2 + lax.rem(where_ref[2] + t, 2) for s in steps for t in range(2)]
    return [pl.ds(pl.multiple_of(p * rows_j, rows_j), rows_j) for p in at]


def first_kernel(half, head_dim, scale_q, steps, n_z, n_now, where_ref, own_ref, other_ref, live_ref, w_in_ref, w_dm_ref, *refs):
    bias_refs, refs = refs[:n_now], refs[n_now:]
    (qd_ref, kv_ref, kvm_ref, ge_ref, dqg_ref, mix_ref, dkv_ref), refs = refs[:7], refs[7:]
    out_refs, (qd_s, ge_s), dbias_refs = refs[:n_now], refs[n_now : n_now + 2], refs[n_now + 2 :]
    clear(dbias_refs)
    weights = (w_in_ref[...], w_dm_ref[...])
    first = where_ref[0] == 0
    rows_j = bias_refs[0].shape[1] // 2
    now = slice(0, dqg_ref.shape[1])
    at = places(where_ref, steps, n_z, rows_j)
    rows = []
    for r in range(qd_ref.shape[0]):
        qd, kv, kvm, ge = project(half, scale_q, first, own_ref[:, r], other_ref[:, r], live_ref[...], *weights)
        kv_ref[r] = kv
        kvm_ref[r] = kvm
        qd_s[r] = qd
        ge_s[r] = ge
        for n, p in enumerate(at):
            here = slice(n * rows_j, (n + 1) * rows_j)
            qd_ref[r, here] = qd_s[r, p]
            ge_ref[r, here] = ge_s[r, p]
        rows.append((qd_ref[r, now], ge_ref[r, now], kv, kvm))
    for r, (dqg, mixed, dkv) in enumerate(attend(half, head_dim, scale_q, rows, bias_refs, dbias_refs)):
        dqg_ref[r] = dqg
        dkv_ref[r] = dkv
        mix_ref[r] = mixed.astype(BF16)
    hand_over(dbias_refs, out_refs)


def middle_kernel(half, head_dim, scale_q, where_ref, qd_ref, kv_ref, kvm_ref, ge_ref, bias_ref, dkv_in_ref, before_ref, *refs):
    dqg_ref, mix_ref, dkv_ref, out_ref, dbias_ref = refs
    clear([dbias_ref])
    rows = [(qd_ref[r], ge_ref[r], kv_ref[r], kvm_ref[r]) for r in range(qd_ref.shape[0])]
    for r, (dqg, mixed, dkv) in enumerate(attend(half, head_dim, scale_q, rows, [bias_ref], [dbias_ref])):
        dqg_ref[r] = dqg
        dkv_ref[r] = dkv_in_ref[r] + dkv
        mix_ref[r] = mixed.astype(BF16)
    hand_over([dbias_ref], [out_ref])


def last_kernel(half, head_dim, scale_q, steps, n_z, where_ref, qd_ref, kv_ref, kvm_ref, ge_ref, bias_ref, dqg_ref, mix_ref, dqg2_ref, mix2_ref, dkv_ref, w_back_ref, *refs):
    (keep_dn_ref, give_dn_ref, keep_mix_ref, give_mix_ref, dbias_ref, dn_s, mix_s) = refs
    clear([dbias_ref])
    rows = [(qd_ref[r], ge_ref[r], kv_ref[r], kvm_ref[r]) for r in range(qd_ref.shape[0])]
    results = attend(half, head_dim, scale_q, rows, [bias_ref], [dbias_ref])
    first = where_ref[0] == 0
    w_back = w_back_ref[...]
    rows_j = bias_ref.shape[1] // 2
    at = places(where_ref, steps, n_z, rows_j)
    chips, _, cells, width = keep_dn_ref.shape
    for r, (dqg, mixed, dkv) in enumerate(results):
        dn_s[r] = dot_exact((dkv + dkv_ref[r]).T, w_back[2 * half :])
        from_queries = dot_exact(jnp.concatenate([dqg_ref[r], dqg2_ref[r], dqg], axis=0), w_back[: 2 * half])
        mixed = jnp.concatenate([mix_ref[r].astype(F32), mix2_ref[r].astype(F32), mixed], axis=0)
        mixed = jnp.where(first, pltpu.roll(mixed, half, 1), mixed)
        for n, p in enumerate(at):
            here = slice(n * rows_j, (n + 1) * rows_j)
            dn_s[r, p] += from_queries[here]
            mix_s[r, p] = mixed[here]
        d_normed = dn_s[r].reshape(chips, 2, cells, width)
        mixed = mix_s[r].reshape(chips, 2, cells, width)
        keep_dn_ref[:, r] = jnp.where(first, d_normed[:, 0], d_normed[:, 1])
        give_dn_ref[:, r] = jnp.where(first, d_normed[:, 1], d_normed[:, 0])
        keep_mix_ref[:, r] = jnp.where(first, mixed[:, 0], mixed[:, 1]).astype(BF16)
        give_mix_ref[:, r] = jnp.where(first, mixed[:, 1], mixed[:, 0]).astype(BF16)


def merge_kernel(keep_dn_ref, came_dn_ref, keep_mix_ref, came_mix_ref, out_ref):
    chips, rows, cells, width = keep_dn_ref.shape
    both = (keep_dn_ref[...] + came_dn_ref[...], keep_mix_ref[...].astype(F32) + came_mix_ref[...].astype(F32))
    lane = lanes((cells, width))
    for n, values in enumerate(both):
        at = slice(n * width, (n + 1) * width)
        codes, quarters = encode(values)
        out_ref[:, :rows, :, at] = codes
        for c in range(chips):
            line = jnp.broadcast_to(quarters[c, 0], (cells, width))
            for r in range(1, rows):
                line = jnp.where(lane == r, quarters[c, r], line)
            out_ref[c, rows, :, at] = line.astype(jnp.int32).astype(jnp.int16)


def finish_kernel(pair_ref, came_ref, dbias_ref, w_out_ref, w_spread_ref, update_ref, dpair_ref, dbias_s):
    rows, cells, width = pair_ref.shape
    chips, chip_rows = came_ref.shape[0], came_ref.shape[1] - 1
    flat = (rows * cells, width)
    lanes_of_head = w_spread_ref.shape[0] // 4
    step = pl.program_id(0)

    @pl.when(step == 0)
    def _():
        for c in range(2):
            total = dbias_ref[c].astype(F32)
            for n in range(c + 2, dbias_ref.shape[0], 2):
                total = total + dbias_ref[n].astype(F32)
            dbias_s[:, c * width : (c + 1) * width] = total

    normed, inverse = normalize(pair_ref[...].reshape(flat))
    lane = lanes((cells, width))
    came = []
    for n in range(2):
        at = slice(n * width, (n + 1) * width)
        quarters = []
        for c in range(chips):
            line = came_ref[c, chip_rows, :, at].astype(jnp.int32).astype(F32)
            quarters += [jnp.sum(jnp.where(lane == r, line, 0.0), axis=-1, keepdims=True) for r in range(chip_rows)]
        came.append(decode(came_ref[:, :chip_rows, :, at].reshape(flat), jnp.concatenate(quarters, axis=0)))
    update_ref[...] = dot(came[1].astype(BF16), w_out_ref[...]).reshape(pair_ref.shape)
    d_bias = dbias_s[...]
    own = lax.rem(lanes(d_bias.shape), lanes_of_head)
    picked = [jnp.where(own == step * rows + r, d_bias, 0.0) for r in range(rows)]
    picked = jnp.concatenate(picked, axis=0)
    from_bias = jnp.zeros(flat, F32)
    for _ in range(3):
        high = picked.astype(BF16)
        from_bias = from_bias + dot(high, w_spread_ref[...])
        picked = picked - high.astype(F32)
    d_normed = came[0] + from_bias
    first_mean = jnp.mean(d_normed, axis=-1, keepdims=True)
    second_mean = jnp.mean(d_normed * normed, axis=-1, keepdims=True)
    dpair_ref[...] = (inverse * (d_normed - first_mean - normed * second_mean)).reshape(pair_ref.shape)


def shifted(array, axis, step):
    size = lax.axis_size(axis)
    return lax.ppermute(array, axis, [(s, (s + step) % size) for s in range(size)])


def kernel(fn, grid, in_specs, out_specs, out_shape, micros, name, scalars=0, scratch=(), aliases=None, vmem=24):
    return pl.pallas_call(
        fn,
        grid_spec=pltpu.PrefetchScalarGridSpec(
            num_scalar_prefetch=scalars, grid=grid, in_specs=in_specs, out_specs=out_specs, scratch_shapes=scratch
        ),
        out_shape=out_shape,
        input_output_aliases=aliases or {},
        compiler_params=pltpu.CompilerParams(vmem_limit_bytes=vmem * 1024 * 1024),
        cost_estimate=pl.CostEstimate(flops=int(micros * 1.1e9), bytes_accessed=int(micros * 2e6), transcendentals=0),
        name=name,
    )


def body(pair_act, token_mask, w_proj, w_bias, w_out, cotangent):
    rows, cells, width = pair_act.shape
    n_heads = w_bias.shape[1]
    head_dim = w_proj.shape[2] // n_heads
    my_heads = n_heads // 2
    half = my_heads * head_dim
    scale_q = 1.0 / math.sqrt(head_dim)
    nx, nyl, nz = (lax.axis_size(a) for a in ("x", "yl", "z"))
    chips = nx * nyl
    own_rows = rows // chips
    n_tokens = chips * 2 * cells
    core, z_at, yh_at = lax.axis_index("c"), lax.axis_index("z"), lax.axis_index("yh")
    cell_at = lax.axis_index(CELL)
    where = jnp.stack([core, z_at, yh_at])
    shape = jax.ShapeDtypeStruct

    def fixed(dims):
        return pl.BlockSpec(dims, lambda r, *w: (0,) * len(dims))

    def by_rows(count):
        return pl.BlockSpec((count * own_rows, cells, width), lambda r: (r, 0, 0))
    anywhere = pl.BlockSpec(memory_space=pl.ANY)

    live_here = lax.dynamic_slice_in_dim(token_mask, cell_at * cells, cells)
    live_here = jnp.broadcast_to(live_here[:, None], (cells, width))
    w_spread = jnp.repeat(w_bias, rows, axis=1)
    n_cells = chips * 2
    vmem = pl.BlockSpec(memory_space=pltpu.VMEM)
    cells_of = (2 * n_cells, cells, my_heads * rows)
    sent, bias = kernel(
        prepare_kernel, (chips // GP,),
        [by_rows(GP)] * 2 + [fixed(live_here.shape), fixed(w_spread.shape)],
        [pl.BlockSpec((GP, own_rows, cells, 2 * width), lambda r: (r, 0, 0, 0)), fixed(cells_of)],
        [shape((chips, own_rows, cells, 2 * width), BF16), shape(cells_of, F32)],
        3, "prepare",
    )(pair_act, cotangent, live_here, w_spread)

    bias = lax.all_to_all(bias, NEAR, 0, 0)
    sent = kernel(
        after_kernel, (), [anywhere, anywhere], anywhere, shape(sent.shape, sent.dtype), 0.1, "after", aliases={0: 0}
    )(sent, bias)
    block_shape = (my_heads, 2 * rows, n_tokens)
    block = kernel(
        turn_kernel, (1,), [fixed((2, n_tokens, my_heads * rows))], fixed(block_shape),
        shape(block_shape, F32), 1, "turn", scalars=1,
    )(where, bias.reshape(2, n_tokens, my_heads * rows))
    order = [1, nz - 1] + list(range(2, nz - 1)) + [0]
    n_now = 2
    bias_of = [shifted(block, "z", nz - s) for s in order[:-1]] + [block]

    w_in, w_back, w_dm = kernel(
        functools.partial(weights_kernel, half), (1,), [fixed(w_proj.shape), fixed(w_out.shape)],
        [fixed((width, 4 * half)), fixed((4 * half, width)), fixed((width, 2 * half))],
        [shape((width, 4 * half), BF16), shape((4 * half, width), BF16), shape((width, 2 * half), BF16)],
        1, "weights", scalars=1,
    )(where, w_proj, w_out)
    live = jnp.broadcast_to(token_mask[:, None], (n_tokens, 2 * half))

    own = lax.all_to_all(sent, CHIP, 0, 0)
    own = kernel(
        after_kernel, (), [anywhere] * 5, anywhere, shape(own.shape, own.dtype), 0.1, "after_own", aliases={0: 0}
    )(own, *bias_of[:n_now], w_in, live)
    other = shifted(own, "c", 1)

    lane_shape = (own_rows, n_tokens, 2 * half)
    n_first = n_now * 2 * rows
    first_shape = (own_rows, n_first, 2 * half)
    cell_shape = (chips, own_rows, cells, width)
    blocks = [fixed(block_shape)] * n_now
    block_out = shape(block_shape, F32)
    coded_shape = block_shape[:2] + (n_tokens + 128,)
    coded_out = shape(coded_shape, jnp.int16)

    def of_rows(count, tokens, at=0):
        return pl.BlockSpec((count, tokens, 2 * half), lambda r, w: (r, at, 0))

    def of_cells(count, lanes_here):
        return pl.BlockSpec((chips, count, cells, lanes_here), lambda r, w: (0, r, 0, 0))

    def dkv_of(count):
        return pl.BlockSpec((count, 2 * half, n_tokens), lambda r, w: (r, 0, 0))

    qd, kv, kvm, ge, dqg, mix, dkv, *d_bias = kernel(
        functools.partial(first_kernel, half, head_dim, scale_q, order, nz, n_now), (own_rows // RA,),
        [of_cells(RA, 2 * width)] * 2 + [fixed(live.shape), fixed(w_in.shape), fixed(w_dm.shape)] + blocks,
        [of_rows(RA, n_tokens)] * 4 + [of_rows(RA, n_first)] * 2 + [dkv_of(RA)] + [fixed(coded_shape)] * n_now,
        [shape(lane_shape, t) for t in (BF16, BF16, BF16, F32)]
        + [shape(first_shape, t) for t in (F32, BF16)]
        + [shape((own_rows, 2 * half, n_tokens), F32)]
        + [coded_out] * n_now,
        20, "first", scalars=1, vmem=60, scratch=[pltpu.VMEM((RA, n_tokens, 2 * half), t) for t in (BF16, F32)] + [pltpu.VMEM(block_shape, F32)] * n_now,
    )(where, own, other, live, w_in, w_dm, *bias_of[:n_now])
    came = [shifted(d, "z", s) for d, s in zip(d_bias, order)]
    one_block = n_tokens - n_first - 2 * rows
    middle = of_rows(RB, one_block, n_first // one_block)
    block_rows = of_rows(RB, one_block)
    block_of_rows = (own_rows, one_block, 2 * half)
    dqg2, mix2, dkv, d_far = kernel(
        functools.partial(middle_kernel, half, head_dim, scale_q), (own_rows // RB,),
        [middle, of_rows(RB, n_tokens), of_rows(RB, n_tokens), middle, fixed(block_shape), dkv_of(RB), anywhere],
        [block_rows, block_rows, dkv_of(RB), fixed(coded_shape)],
        [shape(block_of_rows, F32), shape(block_of_rows, BF16), shape(dkv.shape, F32), coded_out],
        0.1, "middle", scalars=1, vmem=60, scratch=[pltpu.VMEM(block_shape, F32)],
    )(where, qd, kv, kvm, ge, bias_of[2], dkv, kv)
    far = shifted(d_far, "z", order[2])
    last = of_rows(RB, one_block, n_first // one_block + 1)
    keep_dn, give_dn, keep_mix, give_mix, d_here = kernel(
        functools.partial(last_kernel, half, head_dim, scale_q, order, nz), (own_rows // RB,),
        [last, of_rows(RB, n_tokens), of_rows(RB, n_tokens), last, fixed(block_shape)]
        + [of_rows(RB, n_first)] * 2 + [block_rows] * 2 + [dkv_of(RB), fixed(w_back.shape)],
        [of_cells(RB, width)] * 4 + [fixed(block_shape)],
        [shape(cell_shape, t) for t in (F32, F32, BF16, BF16)] + [block_out],
        0.1, "last", scalars=1, vmem=60,
        scratch=[pltpu.VMEM((RB, n_tokens, 2 * half), F32)] * 2,
    )(where, qd, kv, kvm, ge, bias_of[3], dqg, mix, dqg2, mix2, dkv, w_back)

    by_yh = (2, n_cells, cells, my_heads * rows)
    d_bias = kernel(
        turn_back_kernel, (1,), [fixed(block_shape)] + [fixed(coded_shape)] * (nz - 1), fixed(by_yh), shape(by_yh, F32),
        1, "turn_back", scalars=1,
    )(where, d_here, *came, far)
    d_bias = lax.all_to_all(d_bias.reshape(cells_of), NEAR, 0, 0)

    give_dn, give_mix = kernel(
        after_kernel, (), [anywhere] * 5, [anywhere] * 2,
        [shape(cell_shape, F32), shape(cell_shape, BF16)], 0.1, "after_give", aliases={0: 0, 1: 1},
    )(give_dn, give_mix, far, *came)
    came_dn, came_mix = shifted(give_dn, "c", 1), shifted(give_mix, "c", 1)
    cell_block = pl.BlockSpec((GM, own_rows, cells, width), lambda r: (r, 0, 0, 0))

    def wide_block(count):
        return pl.BlockSpec((count, own_rows + 1, cells, 2 * width), lambda r: (r, 0, 0, 0))

    merged = kernel(
        merge_kernel, (chips // GM,), [cell_block] * 4, wide_block(GM),
        shape((chips, own_rows + 1, cells, 2 * width), jnp.int16), 2, "merge",
    )(keep_dn, came_dn, keep_mix, came_mix)
    merged = kernel(
        after_kernel, (), [anywhere] * 2, anywhere, shape(merged.shape, merged.dtype), 0.1, "after_merge", aliases={0: 0}
    )(merged, d_bias)
    back = lax.all_to_all(merged, CHIP, 0, 0)

    return kernel(
        finish_kernel, (chips // GF,),
        [by_rows(GF), wide_block(GF), fixed(cells_of), fixed(w_out.shape), fixed((n_heads * rows, width))],
        [by_rows(GF)] * 2,
        [shape(pair_act.shape, F32)] * 2,
        3, "finish", scratch=[pltpu.VMEM((cells, n_heads * rows), F32)],
    )(pair_act, back, d_bias, w_out, w_spread.T)


def solution(mesh):
    fine = Mesh(mesh.devices.reshape(4, 2, 4, 2, 2), ("z", "yh", "x", "yl", "c"))
    cells = P(("z", "yh"), CELL, None)
    return jax.shard_map(
        body,
        mesh=fine,
        in_specs=(cells, P(), P(), P(), P(), cells),
        out_specs=(cells, cells),
        check_vma=False,
    )
```

profile of v0, /device:TPU:0, one launch (start us, length us, event | category | flops | bytes accessed | tf_op | source)
XLA Modules:
  0.0 133.6 jit_solution(1010185770138182145)
XLA Ops:
  0.6 0.7 broadcast_in_dim.7
  1.3 0.1 copy.13.w_spread_ref
  1.4 0.8 dynamic_slice.3
  2.2 0.1 broadcast_in_dim.6.live_ref
  2.3 1.2 copy-done.9
  3.5 1.0 copy-done.12
  4.6 2.0 %prepare.1 = (bf16[8,8,32,256]{3,2,1,0:T(8,128)(2,1)}, f32[32,32,128]{2,1,0:T(8,128)S(1)}) custom-call(f32[64,32,128]{2,1,0:T(8,128)S(1)} %copy-done.9, bf16[64,32,128]{2,1,0:T(8,128)(2,1)S(1)} %copy-done.12, s32[32,128]{1,0:T(8,128)S(1)} %broadcast_in_dim.6.live_ref, bf16[128,256]{1,0:T(8,128)(2,1)S(1)} %copy.13.w_spread_ref), custom_call_target="tpu_custom_call" | custom-call | flops 3300000000 | bytes 6000000 | tf_op jit(solution)/shard_map/prepare/pallas_call | solution.py:384
  6.6 19.5 %all_to_all.20.refs_1_ = f32[32,32,128]{2,1,0:T(8,128)S(1)} all-to-all(f32[32,32,128]{2,1,0:T(8,128)S(1)} %get-tuple-element.28), channel_id=1, replica_groups=mesh['z'=4,'yh'=2,'x'=4,'yl'=2,'c'=2] {'yh','x','yl','c'}, dimensions={0} | all-to-all | bytes 1048576 | tf_op jit(solution)/shard_map/all_to_all | solution.py:392
  26.1 3.6 %all-to-all-start.1 = ((bf16[8,8,32,256]{3,2,1,0:T(8,128)(2,1)}), bf16[8,8,32,256]{3,2,1,0:T(8,128)(2,1)S(1)}, u32[]{:S(2)}, u32[]{:S(2)}) async-start(bf16[8,8,32,256]{3,2,1,0:T(8,128)(2,1)} %after.1), calls=%async_computation.1 | async-start | bytes 2097152 | tf_op jit(solution)/shard_map/all_to_all | solution.py:413
  29.6 0.0 copy-start.15
  29.6 0.0 copy-start.16
  29.7 0.1 pad_add_fusion.where_ref
  29.7 0.7 turn.1.bias_ref
  30.5 0.0 copy-start.18
  30.5 2.0 %collective-permute-start.1 = (f32[2,128,512]{2,1,0:T(8,128)S(1)}, f32[2,128,512]{2,1,0:T(8,128)S(1)}, u32[]{:S(2)}, u32[]{:S(2)}) collective-permute-start(f32[2,128,512]{2,1,0:T(8,128)S(1)} %turn.1.bias_ref), channel_id=1, source_target_pairs={{0,32},{32,64},{64,96},{96,0},{1,33},{33,65},{65,97},{97,1},{2,34}... | collective-permute-start | bytes 1572872 | tf_op jit(solution)/shard_map/ppermute | solution.py:338
  32.5 2.2 %collective-permute-start = (f32[2,128,512]{2,1,0:T(8,128)S(1)}, f32[2,128,512]{2,1,0:T(8,128)S(1)}, u32[]{:S(2)}, u32[]{:S(2)}) collective-permute-start(f32[2,128,512]{2,1,0:T(8,128)S(1)} %turn.1.bias_ref), channel_id=1, source_target_pairs={{0,96},{32,0},{64,32},{96,64},{1,97},{33,1},{65,33},{97,65},{2,98}... | collective-permute-start | bytes 1572872 | tf_op jit(solution)/shard_map/ppermute | solution.py:338
  34.7 0.9 weights.1
  35.6 0.6 copy-done.5
  36.3 0.6 copy-done.17
  36.9 9.6 %collective-permute-done.1.refs_2_.refs_1_ = f32[2,128,512]{2,1,0:T(8,128)S(1)} collective-permute-done((f32[2,128,512]{2,1,0:T(8,128)S(1)}, f32[2,128,512]{2,1,0:T(8,128)S(1)}, u32[]{:S(2)}, u32[]{:S(2)}) %collective-permute-start.1) | collective-permute-done | bytes 524320 | tf_op jit(solution)/shard_map/ppermute | solution.py:338
  46.5 0.0 collective-permute-done.refs_1_.refs_0_
  46.5 0.0 all-to-all-done.1.refs_0_
  46.5 0.1 broadcast_in_dim.8.refs_4_.live_ref
  46.6 0.0 copy-start
  46.6 0.1 collective-permute-start.2
  46.7 3.3 %collective-permute-start.3 = (f32[2,128,512]{2,1,0:T(8,128)S(1)}, f32[2,128,512]{2,1,0:T(8,128)}, u32[]{:S(2)}, u32[]{:S(2)}) collective-permute-start(f32[2,128,512]{2,1,0:T(8,128)S(1)} %turn.1.bias_ref), channel_id=1, source_target_pairs={{0,64},{32,96},{64,0},{96,32},{1,65},{33,97},{65,1},{97,33},{2,66}... | collective-permute-start | bytes 1572872 | tf_op jit(solution)/shard_map/ppermute | solution.py:338
  50.0 0.0 collective-permute-done.2.other_ref
  50.1 1.0 copy-done.19
  51.0 13.7 %first.1 = (bf16[8,512,128]{2,1,0:T(8,128)(2,1)}, bf16[8,512,128]{2,1,0:T(8,128)(2,1)}, bf16[8,512,128]{2,1,0:T(8,128)(2,1)}, f32[8,512,128]{2,1,0:T(8,128)}, f3...) custom-call(s32[3]{0:T(128)} %copy-done.7, ...), custom_call_target="tpu_custom_call" | custom-call | flops 22000001024 | bytes 40000000 | tf_op jit(solution)/shard_map/first/pallas_call | solution.py:437
  64.8 1.1 collective-permute-start.5
  65.8 2.2 %collective-permute-start.6 = (s16[2,128,640]{2,1,0:T(8,128)(2,1)}, s16[2,128,640]{2,1,0:T(8,128)(2,1)S(1)}, u32[]{:S(2)}, u32[]{:S(2)}) collective-permute-start(s16[2,128,640]{2,1,0:T(8,128)(2,1)} %get-tuple-element.47), channel_id=1, source_target_pairs={{0,96},{32,0},{64,32},{96,64},{1,97},{33,1},{65,33},{97,65},{2,98}... | collective-permute-start | bytes 983048 | tf_op jit(solution)/shard_map/ppermute | solution.py:338
  68.1 0.0 collective-permute-done.3.bias_ref
  68.1 9.1 %middle.1 = (f32[8,128,128]{2,1,0:T(8,128)}, bf16[8,128,128]{2,1,0:T(8,128)(2,1)}, f32[8,128,512]{2,1,0:T(8,128)}, s16[2,128,640]{2,1,0:T(8,128)(2,1)}) custom-call(s32[3]{0:T(128)} %copy-done.7, bf16[8,512,128]{2,1,0:T(8,128)(2,1)} %get-tuple-element.31.qd_ref, bf16[8,512,128]{2,1,0:T(8,128)(2,1)} %get-tuple-element.32.kv_ref.before_ref, ...), custom_call_target="tpu_custom_call" | custom-call | flops 110000000 | bytes 200000 | tf_op jit(solution)/shard_map/middle/pallas_call | solution.py:452
  77.2 1.4 %collective-permute-start.4 = (s16[2,128,640]{2,1,0:T(8,128)(2,1)}, s16[2,128,640]{2,1,0:T(8,128)(2,1)S(1)}, u32[]{:S(2)}, u32[]{:S(2)}) collective-permute-start(s16[2,128,640]{2,1,0:T(8,128)(2,1)} %get-tuple-element.45), channel_id=1, source_target_pairs={{0,64},{32,96},{64,0},{96,32},{1,65},{33,97},{65,1},{97,33},{2,66}... | collective-permute-start | bytes 983048 | tf_op jit(solution)/shard_map/ppermute | solution.py:338
  78.6 10.6 %last.1 = (f32[8,8,32,128]{3,2,1,0:T(8,128)}, f32[8,8,32,128]{3,2,1,0:T(8,128)}, bf16[8,8,32,128]{3,2,1,0:T(8,128)(2,1)}, bf16[8,8,32,128]{3,2,1,0:T(8,128)(2,1)}, f32[2,128,512]{2,1,0:T(8,128)}) custom-call(s32[3]{0:T(128)} %copy-done.7, bf16[8,512,128]{2,1,0:T(8,128)(2,1)} %get-tuple-element.31.qd_ref, ...), custom_call_target="tpu_custom_call" | custom-call | flops 110000000 | bytes 200000 | tf_op jit(solution)/shard_map/last/pallas_call | solution.py:461
  89.2 0.0 collective-permute-done.5.refs_3_.refs_1_
  89.3 0.1 collective-permute-start.7
  89.4 0.5 collective-permute-start.8
  89.9 0.0 copy-done.8
  89.9 0.4 copy-done.14
  90.3 1.7 %turn_back.1 = f32[2,16,32,128]{3,2,1,0:T(8,128)} custom-call(s32[3]{0:T(128)S(1)} %copy-done.8, f32[2,128,512]{2,1,0:T(8,128)S(1)} %copy-done.14, s16[2,128,640]{2,1,0:T(8,128)(2,1)S(1)} %collective-permute-done.5.refs_3_.refs_1_, s16[2,128,640]{2,1,0:T(8,128)(2,1)S(1)} %collective-permute-done.6.refs_4_.refs_2_, ...), custom_call_target="tpu_custom_call" | custom-call | flops 1100000000 | bytes 2000000 | tf_op jit(solution)/shard_map/turn_back/pallas_call | solution.py:472
  92.0 5.6 %all-to-all-start.2 = ((f32[32,32,128]{2,1,0:T(8,128)}), f32[32,32,128]{2,1,0:T(8,128)S(1)}, u32[]{:S(2)}, u32[]{:S(2)}) async-start(f32[32,32,128]{2,1,0:T(8,128)} %bitcast.5), calls=%async_computation.2 | async-start | bytes 1048576 | tf_op jit(solution)/shard_map/all_to_all | solution.py:476
  97.6 0.0 copy-start.11
  97.6 1.2 copy-done.11
  98.9 2.5 %merge.1.refs_0_ = s16[8,9,32,256]{3,2,1,0:T(8,128)(2,1)S(1)} custom-call(f32[8,8,32,128]{3,2,1,0:T(8,128)S(1)} %copy-done.11, f32[8,8,32,128]{3,2,1,0:T(8,128)} %collective-permute-done.7.came_dn_ref, bf16[8,8,32,128]{3,2,1,0:T(8,128)(2,1)S(1)} %copy-done.13, bf16[8,8,32,128]{3,2,1,0:T(8,128)(2,1)S(1)} %collective-permute-done.8.came_mix_ref), custom_call_target="tpu_custom_call" | custom-call | flops 2200000000 | bytes 4000000 | tf_op jit(solution)/shard_map/merge/pallas_call | solution.py:488
  101.4 8.3 %all-to-all-done.2.refs_1_.dbias_ref = f32[32,32,128]{2,1,0:T(8,128)S(1)} async-done(((f32[32,32,128]{2,1,0:T(8,128)}), f32[32,32,128]{2,1,0:T(8,128)S(1)}, u32[]{:S(2)}, u32[]{:S(2)}) %all-to-all-start.2) | async-done | bytes 524320 | tf_op jit(solution)/shard_map/all_to_all | solution.py:476
  109.7 19.7 %all_to_all.21.came_ref = s16[8,9,32,256]{3,2,1,0:T(8,128)(2,1)S(1)} all-to-all(s16[8,9,32,256]{3,2,1,0:T(8,128)(2,1)S(1)} %after_merge.1), channel_id=1, replica_groups=mesh['z'=4,'yh'=2,'x'=4,'yl'=2,'c'=2] {'x','yl'}, dimensions={0} | all-to-all | bytes 2359296 | tf_op jit(solution)/shard_map/all_to_all | solution.py:495
  129.4 4.2 %finish.1 = (f32[64,32,128]{2,1,0:T(8,128)}, f32[64,32,128]{2,1,0:T(8,128)}) custom-call(f32[64,32,128]{2,1,0:T(8,128)S(1)} %copy-done.10, s16[8,9,32,256]{3,2,1,0:T(8,128)(2,1)S(1)} %all_to_all.21.came_ref, f32[32,32,128]{2,1,0:T(8,128)S(1)} %all-to-all-done.2.refs_1_.dbias_ref, bf16[128,128]{1,0:T(8,128)(2,1)S(1)} %copy-done.16, bf16[256,128]{1,0:T(8,128)(2,1)S(1)} %bitcast.10), custom_call_target="tpu_custom_call" | custom-call | flops 3300000000 | bytes 6000000 | tf_op jit(solution)/shard_map/finish/pallas_call | solution.py:497
  (35 shorter events, 0.1 us)
Async XLA Ops:
  2.3 1.2 copy-start.9
  3.5 1.0 copy-start.12
  26.1 20.4 %all-to-all-start.1 = ((bf16[8,8,32,256]{3,2,1,0:T(8,128)(2,1)}), bf16[8,8,32,256]{3,2,1,0:T(8,128)(2,1)S(1)}, u32[]{:S(2)}, u32[]{:S(2)}) async-start(bf16[8,8,32,256]{3,2,1,0:T(8,128)(2,1)} %after.1), calls=%async_computation.1 | async-start | bytes 2097152 | tf_op jit(solution)/shard_map/all_to_all | solution.py:413
  29.6 5.1 %copy-start.15 = (bf16[4,128,128]{2,1,0:T(8,128)(2,1)S(1)}, bf16[4,128,128]{2,1,0:T(8,128)(2,1)}, u32[]{:S(2)}) copy-start(bf16[4,128,128]{2,1,0:T(8,128)(2,1)} %w_proj_ref.1) | copy-start | bytes 393220
  29.6 5.1 %copy-start.16 = (bf16[128,128]{1,0:T(8,128)(2,1)S(1)}, bf16[128,128]{1,0:T(8,128)(2,1)}, u32[]{:S(2)}) copy-start(bf16[128,128]{1,0:T(8,128)(2,1)} %w_out_ref.3) | copy-start | bytes 98308
  29.7 5.9 %copy-start.7 = (s32[3]{0:T(128)}, s32[3]{0:T(128)S(1)}, u32[]{:S(2)}) copy-start(s32[3]{0:T(128)S(1)} %pad_add_fusion.where_ref) | copy-start | bytes 40
  30.5 16.2 %copy-start.2 = (f32[2,128,512]{2,1,0:T(8,128)}, f32[2,128,512]{2,1,0:T(8,128)S(1)}, u32[]{:S(2)}) copy-start(f32[2,128,512]{2,1,0:T(8,128)S(1)} %turn.1.bias_ref) | copy-start | bytes 1572868
  30.5 16.0 %copy-start.18 = (s32[512]{0:T(512)S(1)}, s32[512]{0:T(512)}, u32[]{:S(2)}) copy-start(s32[512]{0:T(512)} %param.7) | copy-start | bytes 6148
  30.5 15.9 %collective-permute-start.1 = (f32[2,128,512]{2,1,0:T(8,128)S(1)}, f32[2,128,512]{2,1,0:T(8,128)S(1)}, u32[]{:S(2)}, u32[]{:S(2)}) collective-permute-start(f32[2,128,512]{2,1,0:T(8,128)S(1)} %turn.1.bias_ref), channel_id=1, source_target_pairs={{0,32},{32,64},{64,96},{96,0},{1,33},{33,65},{65,97},{97,1},{2,34}... | collective-permute-start | bytes 1572872 | tf_op jit(solution)/shard_map/ppermute | solution.py:338
  32.5 14.0 %collective-permute-start = (f32[2,128,512]{2,1,0:T(8,128)S(1)}, f32[2,128,512]{2,1,0:T(8,128)S(1)}, u32[]{:S(2)}, u32[]{:S(2)}) collective-permute-start(f32[2,128,512]{2,1,0:T(8,128)S(1)} %turn.1.bias_ref), channel_id=1, source_target_pairs={{0,96},{32,0},{64,32},{96,64},{1,97},{33,1},{65,33},{97,65},{2,98}... | collective-permute-start | bytes 1572872 | tf_op jit(solution)/shard_map/ppermute | solution.py:338
  35.6 0.6 copy-start.5
  36.3 0.6 copy-start.17
  36.9 14.1 %copy-start.6 = (bf16[128,256]{1,0:T(8,128)(2,1)}, bf16[128,256]{1,0:T(8,128)(2,1)S(1)}, u32[]{:S(2)}) copy-start(bf16[128,256]{1,0:T(8,128)(2,1)S(1)} %get-tuple-element.29.refs_3_.w_in_ref) | copy-start | bytes 196612
  46.5 4.6 %copy-start.3 = (f32[2,128,512]{2,1,0:T(8,128)}, f32[2,128,512]{2,1,0:T(8,128)S(1)}, u32[]{:S(2)}) copy-start(f32[2,128,512]{2,1,0:T(8,128)S(1)} %collective-permute-done.1.refs_2_.refs_1_) | copy-start | bytes 1572868
  46.5 4.6 %copy-start.4 = (f32[2,128,512]{2,1,0:T(8,128)}, f32[2,128,512]{2,1,0:T(8,128)S(1)}, u32[]{:S(2)}) copy-start(f32[2,128,512]{2,1,0:T(8,128)S(1)} %collective-permute-done.refs_1_.refs_0_) | copy-start | bytes 1572868
  46.6 4.4 %copy-start.1 = (s32[512,128]{1,0:T(8,128)}, s32[512,128]{1,0:T(8,128)S(1)}, u32[]{:S(2)}) copy-start(s32[512,128]{1,0:T(8,128)S(1)} %broadcast_in_dim.8.refs_4_.live_ref) | copy-start | bytes 786436
  46.6 4.4 %copy-start = (bf16[8,8,32,256]{3,2,1,0:T(8,128)(2,1)}, bf16[8,8,32,256]{3,2,1,0:T(8,128)(2,1)S(1)}, u32[]{:S(2)}) copy-start(bf16[8,8,32,256]{3,2,1,0:T(8,128)(2,1)S(1)} %after_own.1.own_ref) | copy-start | bytes 3145732
  46.6 3.4 %collective-permute-start.2 = (bf16[8,8,32,256]{3,2,1,0:T(8,128)(2,1)S(1)}, bf16[8,8,32,256]{3,2,1,0:T(8,128)(2,1)S(1)}, u32[]{:S(2)}, u32[]{:S(2)}) collective-permute-start(bf16[8,8,32,256]{3,2,1,0:T(8,128)(2,1)S(1)} %after_own.1.own_ref), channel_id=1, source_target_pairs={{0,1},{1,0},{2,3},{3,2},{4,5},{5,4},{6,7},{7,6},{8,9},{9,8},{10,11... | collective-permute-start | bytes 3145736 | tf_op jit(solution)/shard_map/ppermute | solution.py:338
  46.7 21.3 %collective-permute-start.3 = (f32[2,128,512]{2,1,0:T(8,128)S(1)}, f32[2,128,512]{2,1,0:T(8,128)}, u32[]{:S(2)}, u32[]{:S(2)}) collective-permute-start(f32[2,128,512]{2,1,0:T(8,128)S(1)} %turn.1.bias_ref), channel_id=1, source_target_pairs={{0,64},{32,96},{64,0},{96,32},{1,65},{33,97},{65,1},{97,33},{2,66}... | collective-permute-start | bytes 1572872 | tf_op jit(solution)/shard_map/ppermute | solution.py:338
  50.1 1.0 copy-start.19
  64.8 24.5 %collective-permute-start.5 = (s16[2,128,640]{2,1,0:T(8,128)(2,1)}, s16[2,128,640]{2,1,0:T(8,128)(2,1)S(1)}, u32[]{:S(2)}, u32[]{:S(2)}) collective-permute-start(s16[2,128,640]{2,1,0:T(8,128)(2,1)} %get-tuple-element.46), channel_id=1, source_target_pairs={{0,32},{32,64},{64,96},{96,0},{1,33},{33,65},{65,97},{97,1},{2,34}... | collective-permute-start | bytes 983048 | tf_op jit(solution)/shard_map/ppermute | solution.py:338
  65.8 23.4 %collective-permute-start.6 = (s16[2,128,640]{2,1,0:T(8,128)(2,1)}, s16[2,128,640]{2,1,0:T(8,128)(2,1)S(1)}, u32[]{:S(2)}, u32[]{:S(2)}) collective-permute-start(s16[2,128,640]{2,1,0:T(8,128)(2,1)} %get-tuple-element.47), channel_id=1, source_target_pairs={{0,96},{32,0},{64,32},{96,64},{1,97},{33,1},{65,33},{97,65},{2,98}... | collective-permute-start | bytes 983048 | tf_op jit(solution)/shard_map/ppermute | solution.py:338
  77.2 12.1 %collective-permute-start.4 = (s16[2,128,640]{2,1,0:T(8,128)(2,1)}, s16[2,128,640]{2,1,0:T(8,128)(2,1)S(1)}, u32[]{:S(2)}, u32[]{:S(2)}) collective-permute-start(s16[2,128,640]{2,1,0:T(8,128)(2,1)} %get-tuple-element.45), channel_id=1, source_target_pairs={{0,64},{32,96},{64,0},{96,32},{1,65},{33,97},{65,1},{97,33},{2,66}... | collective-permute-start | bytes 983048 | tf_op jit(solution)/shard_map/ppermute | solution.py:338
  89.2 0.7 copy-start.8
  89.2 1.0 copy-start.14
  89.3 8.3 %collective-permute-start.7 = (f32[8,8,32,128]{3,2,1,0:T(8,128)}, f32[8,8,32,128]{3,2,1,0:T(8,128)}, u32[]{:S(2)}, u32[]{:S(2)}) collective-permute-start(f32[8,8,32,128]{3,2,1,0:T(8,128)} %get-tuple-element.48), channel_id=1, source_target_pairs={{0,1},{1,0},{2,3},{3,2},{4,5},{5,4},{6,7},{7,6},{8,9},{9,8},{10,11... | collective-permute-start | bytes 3145736 | tf_op jit(solution)/shard_map/ppermute | solution.py:338
  89.4 8.2 %collective-permute-start.8 = (bf16[8,8,32,128]{3,2,1,0:T(8,128)(2,1)}, bf16[8,8,32,128]{3,2,1,0:T(8,128)(2,1)S(1)}, u32[]{:S(2)}, u32[]{:S(2)}) collective-permute-start(bf16[8,8,32,128]{3,2,1,0:T(8,128)(2,1)} %get-tuple-element.50), channel_id=1, source_target_pairs={{0,1},{1,0},{2,3},{3,2},{4,5},{5,4},{6,7},{7,6},{8,9},{9,8},{10,11... | collective-permute-start | bytes 1572872 | tf_op jit(solution)/shard_map/ppermute | solution.py:338
  90.3 7.4 %copy-start.13 = (bf16[8,8,32,128]{3,2,1,0:T(8,128)(2,1)S(1)}, bf16[8,8,32,128]{3,2,1,0:T(8,128)(2,1)}, u32[]{:S(2)}) copy-start(bf16[8,8,32,128]{3,2,1,0:T(8,128)(2,1)} %get-tuple-element.49.keep_mix_ref) | copy-start | bytes 1572868
  92.0 17.7 %all-to-all-start.2 = ((f32[32,32,128]{2,1,0:T(8,128)}), f32[32,32,128]{2,1,0:T(8,128)S(1)}, u32[]{:S(2)}, u32[]{:S(2)}) async-start(f32[32,32,128]{2,1,0:T(8,128)} %bitcast.5), calls=%async_computation.2 | async-start | bytes 1048576 | tf_op jit(solution)/shard_map/all_to_all | solution.py:476
  97.6 1.2 copy-start.11
  109.7 19.7 %copy-start.10 = (f32[64,32,128]{2,1,0:T(8,128)S(1)}, f32[64,32,128]{2,1,0:T(8,128)}, u32[]{:S(2)}) copy-start(f32[64,32,128]{2,1,0:T(8,128)} %pair_ref.3) | copy-start | bytes 3145732
where the time goes:
time: 134 us
  Pallas kernels  45.6 us (34%)
  blocking collectives  39.2 us (29%)
  starting transfers between devices  22 us (16%)
  waiting for transfers between devices  17.9 us (13%)
  local copies, waits for them, and re-layouts  7.91 us (6%)
    all_to_all x1, blocking collectives, body(): back = lax.all_to_all(merged, CHIP, 0, 0)  19.7 us
    all_to_all x1, blocking collectives, body(): bias = lax.all_to_all(bias, NEAR, 0, 0)  19.5 us
    pallas_call x1, Pallas kernels, body(): kernel(functools.partial(first_kernel, half, head_dim, scale_q, order, nz...  13.7 us
    ppermute x9, starting transfers between devices, shifted(): lax.ppermute(array, axis, [(s, (s + step) % size) for s in range(size)])  12.9 us
    pallas_call x1, Pallas kernels, body(): kernel(functools.partial(last_kernel, half, head_dim, scale_q, order, nz)...  10.6 us
    ppermute x9, waiting for transfers between devices, shifted(): lax.ppermute(array, axis, [(s, (s + step) % size) for s in range(size)])  9.59 us
    pallas_call x1, Pallas kernels, body(): kernel(functools.partial(middle_kernel, half, head_dim, scale_q), (own_ro...  9.09 us
    all_to_all x1, waiting for transfers between devices, body(): d_bias = lax.all_to_all(d_bias.reshape(cells_of), NEAR, 0, 0)  8.31 us
  transfers between devices with their start and end apart: 11, of which 2 were waited for; matrix products, arithmetic and copies ran while one was open for 0% of the time, Pallas kernels for 29%

commit v1 on v0

--- a/solution.py
+++ b/solution.py
@@ -1,4 +1,5 @@
 import functools
+import itertools
 import math
 
 import jax
@@ -12,7 +13,8 @@
 masked_score = -1000000000.0
 code_top = 32000.0
 RA = 2
-RB = 2
+RB = 4
+RL = 4
 GP = 4
 GM = 4
 GF = 4
@@ -84,17 +86,25 @@
             out_ref[h, t * rows : (t + 1) * rows] = block[h * rows : (h + 1) * rows]
 
 
-def turn_back_kernel(where_ref, *refs):
-    here_ref, *came_refs, out_ref = refs
-    total = here_ref[...]
-    n_tokens = total.shape[-1]
+def far_kernel(own_ref, *refs):
+    *came_refs, out_ref = refs
+    total = own_ref[...]
     for ref in came_refs:
-        quarters = ref[..., n_tokens:].astype(jnp.int32).astype(F32)
-        total = total + decode(ref[..., :n_tokens], jnp.max(quarters, axis=-1, keepdims=True))
-    rows = total.shape[1] // 2
-    for t in range(2):
-        both = total[:, t * rows : (t + 1) * rows].reshape(total.shape[0] * rows, -1)
-        out_ref[lax.rem(where_ref[2] + t, 2)] = both.T.reshape(out_ref.shape[1:])
+        total = total + get_lines(ref, total.shape[-1])[:, total.shape[1] :]
+    put_lines(total, out_ref)
+
+
+def lines_kernel(where_ref, own_ref, *refs):
+    *came_refs, keep_ref, give_ref = refs
+    heads, rows, n_tokens = own_ref.shape
+    chips, cells, _ = keep_ref.shape
+    total = own_ref[...]
+    for ref in came_refs:
+        total = total + get_lines(ref, n_tokens)
+    total = total.reshape(heads * rows, n_tokens).T.reshape(chips, 2, cells, heads * rows)
+    first = where_ref[0] == 0
+    put_lines(jnp.where(first, total[:, 0], total[:, 1]), keep_ref)
+    put_lines(jnp.where(first, total[:, 1], total[:, 0]), give_ref)
 
 
 def weights_kernel(half, where_ref, w_proj_ref, w_out_ref, w_in_ref, w_back_ref, w_dm_ref):
@@ -128,32 +138,44 @@
     return qd, kv, kvm, jnp.where(low, pltpu.roll(gate, half, 1), d_att)
 
 
-def encode(values):
-    most = jnp.maximum(jnp.max(jnp.abs(values), axis=-1, keepdims=True), 1e-30)
-    quarters = jnp.floor(jnp.log(most) * (4.0 / math.log(2.0))) + 2.0
+def exponents(most):
+    return jnp.floor(jnp.log(jnp.maximum(most, 1e-30)) * (4.0 / math.log(2.0))) + 2.0
+
+
+def encode(values, quarters):
     codes = jnp.floor(values * (code_top * jnp.exp2(quarters * -0.25)) + 0.5)
-    return codes.astype(jnp.int32).astype(jnp.int16), quarters
+    return codes.astype(jnp.int32)
 
 
 def decode(codes, quarters):
     return codes.astype(jnp.int32).astype(F32) * (jnp.exp2(quarters * 0.25) * (1.0 / code_top))
+
+
+def put_lines(values, out_ref):
+    size = values.shape[-1]
+    quarters = exponents(jnp.max(jnp.abs(values), axis=-1, keepdims=True))
+    out_ref[..., :size] = encode(values, quarters).astype(jnp.int16)
+    quarters = jnp.broadcast_to(quarters, values.shape[:-1] + (out_ref.shape[-1] - size,))
+    out_ref[..., size:] = quarters.astype(jnp.int32).astype(jnp.int16)
+
+
+def get_lines(ref, size):
+    quarters = ref[..., size:].astype(jnp.int32).astype(F32)
+    return decode(ref[..., :size], jnp.max(quarters, axis=-1, keepdims=True))
 
 
 def hand_over(dbias_refs, out_refs):
     @pl.when(pl.program_id(0) == pl.num_programs(0) - 1)
     def _():
         for ref, out_ref in zip(dbias_refs, out_refs):
-            n_tokens = ref.shape[-1]
-            codes, quarters = encode(ref[...])
-            out_ref[..., :n_tokens] = codes
-            quarters = jnp.broadcast_to(quarters, codes.shape[:-1] + (out_ref.shape[-1] - n_tokens,))
-            out_ref[..., n_tokens:] = quarters.astype(jnp.int32).astype(jnp.int16)
+            put_lines(ref[...], out_ref)
 
 
 def attend(half, head_dim, scale_q, rows, bias_refs, dbias_refs):
     heads = range(half // head_dim)
     each = [(r, h) for r in range(len(rows)) for h in heads]
-    block = bias_refs[0].shape[1]
+    ends = list(itertools.accumulate(ref.shape[1] for ref in bias_refs))
+    cuts = [slice(end - ref.shape[1], end) for end, ref in zip(ends, bias_refs)]
     qds, ges, kvs, kvms = zip(*rows)
     lane = lanes(qds[0].shape)
     zero = jnp.zeros_like(qds[0])
@@ -166,7 +188,7 @@
     qd_t = [qd.astype(F32).T.astype(BF16) for qd in qds]
     attention, low = {}, {}
     for r, h in each:
-        biased = [scores[r, h][n * block : (n + 1) * block] + ref[h] for n, ref in enumerate(bias_refs)]
+        biased = [scores[r, h][cut] + ref[h] for cut, ref in zip(cuts, bias_refs)]
         biased = jnp.concatenate(biased, axis=0)
         weights = jnp.exp(biased - jnp.max(biased, axis=-1, keepdims=True))
         attention[r, h] = weights * (1.0 / jnp.sum(weights, axis=-1, keepdims=True))
@@ -183,8 +205,8 @@
             d_scores = attention[r, h] * (d_probs[r, h] - delta)
             total = d_scores if total is None else total + d_scores
             d_low[r, h] = d_scores.astype(BF16)
-        for n, ref in enumerate(dbias_refs):
-            ref[h] += total[n * block : (n + 1) * block]
+        for cut, ref in zip(cuts, dbias_refs):
+            ref[h] += total[cut]
     results = []
     for r in range(len(rows)):
         gate = pltpu.roll(ges[r], half, 1)
@@ -205,12 +227,12 @@
             ref[...] = jnp.zeros_like(ref)
 
 
-def places(where_ref, steps, n_z, rows_j):
-    at = [lax.rem(where_ref[1] + s, n_z) * 2 + lax.rem(where_ref[2] + t, 2) for s in steps for t in range(2)]
+def places(where_ref, order, n_z, rows_j):
+    at = [lax.rem(where_ref[1] + s, n_z) * 2 + lax.rem(where_ref[2] + t, 2) for s, t in order]
     return [pl.ds(pl.multiple_of(p * rows_j, rows_j), rows_j) for p in at]
 
 
-def first_kernel(half, head_dim, scale_q, steps, n_z, n_now, where_ref, own_ref, other_ref, live_ref, w_in_ref, w_dm_ref, *refs):
+def first_kernel(half, head_dim, scale_q, order, n_z, n_now, where_ref, own_ref, other_ref, live_ref, w_in_ref, w_dm_ref, *refs):
     bias_refs, refs = refs[:n_now], refs[n_now:]
     (qd_ref, kv_ref, kvm_ref, ge_ref, dqg_ref, mix_ref, dkv_ref), refs = refs[:7], refs[7:]
     out_refs, (qd_s, ge_s), dbias_refs = refs[:n_now], refs[n_now : n_now + 2], refs[n_now + 2 :]
@@ -219,7 +241,7 @@
     first = where_ref[0] == 0
     rows_j = bias_refs[0].shape[1] // 2
     now = slice(0, dqg_ref.shape[1])
-    at = places(where_ref, steps, n_z, rows_j)
+    at = places(where_ref, order, n_z, rows_j)
     rows = []
     for r in range(qd_ref.shape[0]):
         qd, kv, kvm, ge = project(half, scale_q, first, own_ref[:, r], other_ref[:, r], live_ref[...], *weights)
@@ -239,26 +261,32 @@
     hand_over(dbias_refs, out_refs)
 
 
-def middle_kernel(half, head_dim, scale_q, where_ref, qd_ref, kv_ref, kvm_ref, ge_ref, bias_ref, dkv_in_ref, before_ref, *refs):
-    dqg_ref, mix_ref, dkv_ref, out_ref, dbias_ref = refs
-    clear([dbias_ref])
-    rows = [(qd_ref[r], ge_ref[r], kv_ref[r], kvm_ref[r]) for r in range(qd_ref.shape[0])]
-    for r, (dqg, mixed, dkv) in enumerate(attend(half, head_dim, scale_q, rows, [bias_ref], [dbias_ref])):
+def middle_kernel(half, head_dim, scale_q, at, where_ref, qd_ref, kv_ref, kvm_ref, ge_ref, far_bias_ref, own_bias_ref, dkv_in_ref, *refs):
+    dqg_ref, mix_ref, dkv_ref, near_ref, far_ref, own_ref, dbias_ref = refs
+    clear([dbias_ref, own_ref])
+    rows = [(qd_ref[r, at], ge_ref[r, at], kv_ref[r], kvm_ref[r]) for r in range(qd_ref.shape[0])]
+    results = attend(half, head_dim, scale_q, rows, [far_bias_ref, own_bias_ref], [dbias_ref, own_ref])
+    for r, (dqg, mixed, dkv) in enumerate(results):
         dqg_ref[r] = dqg
         dkv_ref[r] = dkv_in_ref[r] + dkv
         mix_ref[r] = mixed.astype(BF16)
-    hand_over([dbias_ref], [out_ref])
-
-
-def last_kernel(half, head_dim, scale_q, steps, n_z, where_ref, qd_ref, kv_ref, kvm_ref, ge_ref, bias_ref, dqg_ref, mix_ref, dqg2_ref, mix2_ref, dkv_ref, w_back_ref, *refs):
+
+    @pl.when(pl.program_id(0) == pl.num_programs(0) - 1)
+    def _():
+        rows_j = near_ref.shape[1]
+        put_lines(dbias_ref[:, :rows_j], near_ref)
+        put_lines(dbias_ref[:, rows_j:], far_ref)
+
+
+def last_kernel(half, head_dim, scale_q, order, n_z, where_ref, qd_ref, kv_ref, kvm_ref, ge_ref, bias_ref, dqg_ref, mix_ref, dqg2_ref, mix2_ref, dkv_ref, w_back_ref, *refs):
     (keep_dn_ref, give_dn_ref, keep_mix_ref, give_mix_ref, dbias_ref, dn_s, mix_s) = refs
     clear([dbias_ref])
     rows = [(qd_ref[r], ge_ref[r], kv_ref[r], kvm_ref[r]) for r in range(qd_ref.shape[0])]
     results = attend(half, head_dim, scale_q, rows, [bias_ref], [dbias_ref])
     first = where_ref[0] == 0
     w_back = w_back_ref[...]
-    rows_j = bias_ref.shape[1] // 2
-    at = places(where_ref, steps, n_z, rows_j)
+    rows_j = bias_ref.shape[1]
+    at = places(where_ref, order, n_z, rows_j)
     chips, _, cells, width = keep_dn_ref.shape
     for r, (dqg, mixed, dkv) in enumerate(results):
         dn_s[r] = dot_exact((dkv + dkv_ref[r]).T, w_back[2 * half :])
@@ -277,46 +305,62 @@
         give_mix_ref[:, r] = jnp.where(first, mixed[:, 1], mixed[:, 0]).astype(BF16)
 
 
-def merge_kernel(keep_dn_ref, came_dn_ref, keep_mix_ref, came_mix_ref, out_ref):
+def merge_kernel(where_ref, keep_dn_ref, came_dn_ref, keep_mix_ref, came_mix_ref, keep_lines_ref, came_lines_ref, out_ref):
     chips, rows, cells, width = keep_dn_ref.shape
-    both = (keep_dn_ref[...] + came_dn_ref[...], keep_mix_ref[...].astype(F32) + came_mix_ref[...].astype(F32))
+    d_normed = keep_dn_ref[...] + came_dn_ref[...]
+    d_normed = d_normed - d_normed[..., width - 1 :]
+    mixed = keep_mix_ref[...].astype(F32) + came_mix_ref[...].astype(F32)
+    first = where_ref[0] == 0
+    keep, came = (ref[...].astype(jnp.int32) for ref in (keep_lines_ref, came_lines_ref))
+    lines = (jnp.where(first, keep, came), jnp.where(first, came, keep))
     lane = lanes((cells, width))
-    for n, values in enumerate(both):
-        at = slice(n * width, (n + 1) * width)
-        codes, quarters = encode(values)
-        out_ref[:, :rows, :, at] = codes
-        for c in range(chips):
-            line = jnp.broadcast_to(quarters[c, 0], (cells, width))
-            for r in range(1, rows):
-                line = jnp.where(lane == r, quarters[c, r], line)
-            out_ref[c, rows, :, at] = line.astype(jnp.int32).astype(jnp.int16)
-
-
-def finish_kernel(pair_ref, came_ref, dbias_ref, w_out_ref, w_spread_ref, update_ref, dpair_ref, dbias_s):
+    for c in range(chips):
+        scales = []
+        for values in (d_normed, mixed):
+            most = jnp.max(jnp.max(jnp.abs(values[c]), axis=0), axis=-1, keepdims=True)
+            scales.append(jnp.broadcast_to(exponents(most), (cells, width)))
+        slots = [s.astype(jnp.int32) for s in scales] + [line[c, :, width:] for line in lines]
+        for r in range(rows):
+            codes = encode(d_normed[c, r], scales[0])
+            if r < len(slots):
+                codes = jnp.where(lane == width - 1, slots[r], codes)
+            out_ref[c, r, :, :width] = codes.astype(jnp.int16)
+            out_ref[c, r, :, width:] = encode(mixed[c, r], scales[1]).astype(jnp.int16)
+        for n in range(2):
+            out_ref[c, rows, :, n * width : (n + 1) * width] = lines[n][c, :, :width].astype(jnp.int16)
+
+
+def finish_kernel(pair_ref, came_ref, scales_ref, lines_ref, w_out_ref, w_spread_ref, update_ref, dpair_ref, dbias_s):
     rows, cells, width = pair_ref.shape
     chips, chip_rows = came_ref.shape[0], came_ref.shape[1] - 1
     flat = (rows * cells, width)
     lanes_of_head = w_spread_ref.shape[0] // 4
     step = pl.program_id(0)
+    last = lanes((cells, width)) == width - 1
+
+    def slot(line):
+        line = line.astype(jnp.int32).astype(F32)
+        return jnp.sum(jnp.where(last, line, 0.0), axis=-1, keepdims=True)
 
     @pl.when(step == 0)
     def _():
         for c in range(2):
-            total = dbias_ref[c].astype(F32)
-            for n in range(c + 2, dbias_ref.shape[0], 2):
-                total = total + dbias_ref[n].astype(F32)
+            at = slice(c * width, (c + 1) * width)
+            total = jnp.zeros((cells, width), F32)
+            for n in range(lines_ref.shape[0]):
+                total = total + decode(lines_ref[n, 0, :, at], slot(scales_ref[n, c, :, :width]))
             dbias_s[:, c * width : (c + 1) * width] = total
 
     normed, inverse = normalize(pair_ref[...].reshape(flat))
-    lane = lanes((cells, width))
     came = []
     for n in range(2):
-        at = slice(n * width, (n + 1) * width)
-        quarters = []
+        parts = []
         for c in range(chips):
-            line = came_ref[c, chip_rows, :, at].astype(jnp.int32).astype(F32)
-            quarters += [jnp.sum(jnp.where(lane == r, line, 0.0), axis=-1, keepdims=True) for r in range(chip_rows)]
-        came.append(decode(came_ref[:, :chip_rows, :, at].reshape(flat), jnp.concatenate(quarters, axis=0)))
+            scale = slot(came_ref[c, n, :, :width])
+            for r in range(chip_rows):
+                part = decode(came_ref[c, r, :, n * width : (n + 1) * width], scale)
+                parts.append(jnp.where(last, 0.0, part) if n == 0 else part)
+        came.append(jnp.concatenate(parts, axis=0))
     update_ref[...] = dot(came[1].astype(BF16), w_out_ref[...]).reshape(pair_ref.shape)
     d_bias = dbias_s[...]
     own = lax.rem(lanes(d_bias.shape), lanes_of_head)
@@ -398,9 +442,11 @@
         turn_kernel, (1,), [fixed((2, n_tokens, my_heads * rows))], fixed(block_shape),
         shape(block_shape, F32), 1, "turn", scalars=1,
     )(where, bias.reshape(2, n_tokens, my_heads * rows))
-    order = [1, nz - 1] + list(range(2, nz - 1)) + [0]
+    order = [(1, 0), (1, 1), (nz - 1, 0), (nz - 1, 1), (2, 0), (2, 1), (0, 1), (0, 0)]
     n_now = 2
-    bias_of = [shifted(block, "z", nz - s) for s in order[:-1]] + [block]
+    after_it = shifted(block, "z", 1)
+    before_it = shifted(block, "z", nz - 1)
+    bias_of = [before_it, after_it, shifted(block, "z", nz - 2)]
 
     w_in, w_back, w_dm = kernel(
         functools.partial(weights_kernel, half), (1,), [fixed(w_proj.shape), fixed(w_out.shape)],
@@ -413,7 +459,7 @@
     own = lax.all_to_all(sent, CHIP, 0, 0)
     own = kernel(
         after_kernel, (), [anywhere] * 5, anywhere, shape(own.shape, own.dtype), 0.1, "after_own", aliases={0: 0}
-    )(own, *bias_of[:n_now], w_in, live)
+    )(own, bias_of[1], bias_of[0], w_in, live)
     other = shifted(own, "c", 1)
 
     lane_shape = (own_rows, n_tokens, 2 * half)
@@ -444,63 +490,75 @@
         + [coded_out] * n_now,
         20, "first", scalars=1, vmem=60, scratch=[pltpu.VMEM((RA, n_tokens, 2 * half), t) for t in (BF16, F32)] + [pltpu.VMEM(block_shape, F32)] * n_now,
     )(where, own, other, live, w_in, w_dm, *bias_of[:n_now])
-    came = [shifted(d, "z", s) for d, s in zip(d_bias, order)]
-    one_block = n_tokens - n_first - 2 * rows
-    middle = of_rows(RB, one_block, n_first // one_block)
-    block_rows = of_rows(RB, one_block)
-    block_of_rows = (own_rows, one_block, 2 * half)
-    dqg2, mix2, dkv, d_far = kernel(
-        functools.partial(middle_kernel, half, head_dim, scale_q), (own_rows // RB,),
-        [middle, of_rows(RB, n_tokens), of_rows(RB, n_tokens), middle, fixed(block_shape), dkv_of(RB), anywhere],
-        [block_rows, block_rows, dkv_of(RB), fixed(coded_shape)],
-        [shape(block_of_rows, F32), shape(block_of_rows, BF16), shape(dkv.shape, F32), coded_out],
+    came = [shifted(d, "z", s) for d, s in zip(d_bias, (1, nz - 1))]
+    n_middle = 3 * rows
+    middle_rows = of_rows(RB, n_middle)
+    middle_shape = (own_rows, n_middle, 2 * half)
+    half_shape = (my_heads, rows, n_tokens)
+    lines_out = (my_heads, rows, n_tokens + 128)
+    near_half = pl.BlockSpec(half_shape, lambda r, w: (0, 0, 0))
+    far_half = pl.BlockSpec(half_shape, lambda r, w: (0, 1, 0))
+    whole_row = of_rows(RB, n_tokens)
+    dqg2, mix2, dkv, d_near, d_far, d_own = kernel(
+        functools.partial(middle_kernel, half, head_dim, scale_q, slice(n_first, n_first + n_middle)), (own_rows // RB,),
+        [whole_row] * 4 + [fixed(block_shape), far_half, dkv_of(RB)],
+        [middle_rows, middle_rows, dkv_of(RB), fixed(lines_out), fixed(lines_out), fixed(half_shape)],
+        [shape(middle_shape, F32), shape(middle_shape, BF16), shape(dkv.shape, F32)]
+        + [shape(lines_out, jnp.int16)] * 2 + [shape(half_shape, F32)],
         0.1, "middle", scalars=1, vmem=60, scratch=[pltpu.VMEM(block_shape, F32)],
-    )(where, qd, kv, kvm, ge, bias_of[2], dkv, kv)
-    far = shifted(d_far, "z", order[2])
-    last = of_rows(RB, one_block, n_first // one_block + 1)
+    )(where, qd, kv, kvm, ge, bias_of[2], block, dkv)
+    across = [(s, (s // 2 + 2) % nz * 2 + 1 - s % 2) for s in range(2 * nz)]
+    came_near, came_far = shifted(d_near, "z", 2), lax.ppermute(d_far, ("z", "yh"), across)
+    d_own = kernel(
+        far_kernel, (1,), [fixed(half_shape)] + [fixed(coded_shape)] * 2, fixed(lines_out), shape(lines_out, jnp.int16),
+        0.1, "far",
+    )(d_own, *came)
+    came_own = shifted(d_own, "yh", 1)
+    last = of_rows(RL, rows, n_tokens // rows - 1)
     keep_dn, give_dn, keep_mix, give_mix, d_here = kernel(
-        functools.partial(last_kernel, half, head_dim, scale_q, order, nz), (own_rows // RB,),
-        [last, of_rows(RB, n_tokens), of_rows(RB, n_tokens), last, fixed(block_shape)]
-        + [of_rows(RB, n_first)] * 2 + [block_rows] * 2 + [dkv_of(RB), fixed(w_back.shape)],
-        [of_cells(RB, width)] * 4 + [fixed(block_shape)],
-        [shape(cell_shape, t) for t in (F32, F32, BF16, BF16)] + [block_out],
+        functools.partial(last_kernel, half, head_dim, scale_q, order, nz), (own_rows // RL,),
+        [last, of_rows(RL, n_tokens), of_rows(RL, n_tokens), last, near_half]
+        + [of_rows(RL, n_first)] * 2 + [of_rows(RL, n_middle)] * 2 + [dkv_of(RL), fixed(w_back.shape)],
+        [of_cells(RL, width)] * 4 + [fixed(half_shape)],
+        [shape(cell_shape, t) for t in (F32, F32, BF16, BF16)] + [shape(half_shape, F32)],
         0.1, "last", scalars=1, vmem=60,
-        scratch=[pltpu.VMEM((RB, n_tokens, 2 * half), F32)] * 2,
-    )(where, qd, kv, kvm, ge, bias_of[3], dqg, mix, dqg2, mix2, dkv, w_back)
-
-    by_yh = (2, n_cells, cells, my_heads * rows)
-    d_bias = kernel(
-        turn_back_kernel, (1,), [fixed(block_shape)] + [fixed(coded_shape)] * (nz - 1), fixed(by_yh), shape(by_yh, F32),
-        1, "turn_back", scalars=1,
-    )(where, d_here, *came, far)
-    d_bias = lax.all_to_all(d_bias.reshape(cells_of), NEAR, 0, 0)
+        scratch=[pltpu.VMEM((RL, n_tokens, 2 * half), F32)] * 2,
+    )(where, qd, kv, kvm, ge, block, dqg, mix, dqg2, mix2, dkv, w_back)
+
+    lines_shape = (chips, cells, 2 * width)
+    keep_lines, give_lines = kernel(
+        lines_kernel, (1,), [fixed(half_shape)] + [fixed(lines_out)] * 5, [fixed(lines_shape)] * 2,
+        [shape(lines_shape, jnp.int16)] * 2, 1, "lines", scalars=1,
+    )(where, d_here, *came, came_near, came_far, came_own)
+    came_lines = shifted(give_lines, "c", 1)
 
     give_dn, give_mix = kernel(
         after_kernel, (), [anywhere] * 5, [anywhere] * 2,
         [shape(cell_shape, F32), shape(cell_shape, BF16)], 0.1, "after_give", aliases={0: 0, 1: 1},
-    )(give_dn, give_mix, far, *came)
+    )(give_dn, give_mix, came_near, came_far, came_own)
     came_dn, came_mix = shifted(give_dn, "c", 1), shifted(give_mix, "c", 1)
-    cell_block = pl.BlockSpec((GM, own_rows, cells, width), lambda r: (r, 0, 0, 0))
+    cell_block = pl.BlockSpec((GM, own_rows, cells, width), lambda r, w: (r, 0, 0, 0))
+    line_block = pl.BlockSpec((GM, cells, 2 * width), lambda r, w: (r, 0, 0))
 
     def wide_block(count):
-        return pl.BlockSpec((count, own_rows + 1, cells, 2 * width), lambda r: (r, 0, 0, 0))
+        return pl.BlockSpec((count, own_rows + 1, cells, 2 * width), lambda r, *w: (r, 0, 0, 0))
 
     merged = kernel(
-        merge_kernel, (chips // GM,), [cell_block] * 4, wide_block(GM),
-        shape((chips, own_rows + 1, cells, 2 * width), jnp.int16), 2, "merge",
-    )(keep_dn, came_dn, keep_mix, came_mix)
-    merged = kernel(
-        after_kernel, (), [anywhere] * 2, anywhere, shape(merged.shape, merged.dtype), 0.1, "after_merge", aliases={0: 0}
-    )(merged, d_bias)
+        merge_kernel, (chips // GM,), [cell_block] * 4 + [line_block] * 2, wide_block(GM),
+        shape((chips, own_rows + 1, cells, 2 * width), jnp.int16), 2, "merge", scalars=1,
+    )(where, keep_dn, came_dn, keep_mix, came_mix, keep_lines, came_lines)
     back = lax.all_to_all(merged, CHIP, 0, 0)
+
+    def rows_of(count, at):
+        return pl.BlockSpec((chips, count, cells, 2 * width), lambda r: (0, at, 0, 0))
 
     return kernel(
         finish_kernel, (chips // GF,),
-        [by_rows(GF), wide_block(GF), fixed(cells_of), fixed(w_out.shape), fixed((n_heads * rows, width))],
+        [by_rows(GF), wide_block(GF), rows_of(2, 1), rows_of(1, own_rows), fixed(w_out.shape), fixed((n_heads * rows, width))],
         [by_rows(GF)] * 2,
         [shape(pair_act.shape, F32)] * 2,
         3, "finish", scratch=[pltpu.VMEM((cells, n_heads * rows), F32)],
-    )(pair_act, back, d_bias, w_out, w_spread.T)
+    )(pair_act, back, back, back, w_out, w_spread.T)
 
 
 def solution(mesh):

time: 134 us -> 127 us (0.948)
  waiting for transfers between devices: 17.9 us -> 11.5 us
  Pallas kernels: 45.6 us -> 42.9 us
  blocking collectives: 39.2 us -> 41.6 us
    all_to_all x1 -> x0, waiting for transfers between devices: 8.31 us -> none  [body(): d_bias = lax.all_to_all(d_bias.reshape(cells_of), NEAR, 0, 0)]
    all_to_all x1 -> x0, starting transfers between devices: 5.58 us -> none  [body(): d_bias = lax.all_to_all(d_bias.reshape(cells_of), NEAR, 0, 0)]
    ppermute x9 -> x11, starting transfers between devices: 12.9 us -> 16.1 us  [shifted(): lax.ppermute(array, axis, [(s, (s + step) % size) for s in range(size)])]
    all_to_all x1, blocking collectives: 19.7 us -> 22.2 us  [body(): back = lax.all_to_all(merged, CHIP, 0, 0)]
    ppermute x0 -> x1, starting transfers between devices: none -> 2.42 us  [body(): lax.ppermute(d_far, ('z', 'yh'), across)]
    ppermute x9 -> x11, waiting for transfers between devices: 9.59 us -> 11.5 us  [shifted(): lax.ppermute(array, axis, [(s, (s + step) % size) for s in range(size)])]
    pallas_call x1, Pallas kernels: 10.6 us -> 9.24 us  [body(): kernel(functools.partial(last_kernel, half, head_dim, scale_q, order, nz)...]
    unnamed x40 -> x42, local copies, waits for them, and re-layouts: 6.15 us -> 5.84 us
  transfers between devices with their start and end apart: 11 -> 13, of which waited for: 2 -> 2; matrix products, arithmetic and copies ran while one was open for 0% -> 0% of each run, Pallas kernels for 29% -> 29%
where the time goes in v1:
time: 127 us
  Pallas kernels  42.9 us (34%)
  blocking collectives  41.6 us (33%)
  starting transfers between devices  22 us (17%)
  waiting for transfers between devices  11.5 us (9%)
  local copies, waits for them, and re-layouts  7.59 us (6%)
    all_to_all x1, blocking collectives, body(): back = lax.all_to_all(merged, CHIP, 0, 0)  22.2 us
    all_to_all x1, blocking collectives, body(): bias = lax.all_to_all(bias, NEAR, 0, 0)  19.5 us
    ppermute x11, starting transfers between devices, shifted(): lax.ppermute(array, axis, [(s, (s + step) % size) for s in range(size)])  16.1 us
    pallas_call x1, Pallas kernels, body(): kernel(functools.partial(first_kernel, half, head_dim, scale_q, order, nz...  13.6 us
    ppermute x11, waiting for transfers between devices, shifted(): lax.ppermute(array, axis, [(s, (s + step) % size) for s in range(size)])  11.5 us
    pallas_call x1, Pallas kernels, body(): kernel(functools.partial(middle_kernel, half, head_dim, scale_q, slice(n_...  10.6 us
    pallas_call x1, Pallas kernels, body(): kernel(functools.partial(last_kernel, half, head_dim, scale_q, order, nz)...  9.24 us
    unnamed x42, local copies, waits for them, and re-layouts  5.84 us
  transfers between devices with their start and end apart: 13, of which 2 were waited for; matrix products, arithmetic and copies ran while one was open for 0% of the time, Pallas kernels for 29%

profile of v1, /device:TPU:0, one launch (start us, length us, event | category | flops | bytes accessed | tf_op | source)
XLA Modules:
  0.0 126.6 jit_solution(167000926585993497)
XLA Ops:
  0.6 0.7 broadcast_in_dim.7
  1.3 0.1 copy.12.w_spread_ref
  1.4 0.8 dynamic_slice.3
  2.2 0.1 broadcast_in_dim.6.live_ref
  2.3 1.2 copy-done.10
  3.5 1.0 copy-done.13
  4.6 2.0 %prepare.1 = (bf16[8,8,32,256]{3,2,1,0:T(8,128)(2,1)}, f32[32,32,128]{2,1,0:T(8,128)S(1)}) custom-call(f32[64,32,128]{2,1,0:T(8,128)S(1)} %copy-done.10, bf16[64,32,128]{2,1,0:T(8,128)(2,1)S(1)} %copy-done.13, s32[32,128]{1,0:T(8,128)S(1)} %broadcast_in_dim.6.live_ref, bf16[128,256]{1,0:T(8,128)(2,1)S(1)} %copy.12.w_spread_ref), custom_call_target="tpu_custom_call" | custom-call | flops 3300000000 | bytes 6000000 | tf_op jit(solution)/shard_map/prepare/pallas_call | solution.py:428
  6.6 19.5 %all_to_all.15.refs_1_ = f32[32,32,128]{2,1,0:T(8,128)S(1)} all-to-all(f32[32,32,128]{2,1,0:T(8,128)S(1)} %get-tuple-element.32), channel_id=1, replica_groups=mesh['z'=4,'yh'=2,'x'=4,'yl'=2,'c'=2] {'yh','x','yl','c'}, dimensions={0} | all-to-all | bytes 1048576 | tf_op jit(solution)/shard_map/all_to_all | solution.py:436
  26.1 3.6 %all-to-all-start.1 = ((bf16[8,8,32,256]{3,2,1,0:T(8,128)(2,1)}), bf16[8,8,32,256]{3,2,1,0:T(8,128)(2,1)S(1)}, u32[]{:S(2)}, u32[]{:S(2)}) async-start(bf16[8,8,32,256]{3,2,1,0:T(8,128)(2,1)} %after.1), calls=%async_computation.1 | async-start | bytes 2097152 | tf_op jit(solution)/shard_map/all_to_all | solution.py:459
  29.6 0.0 copy-start.16
  29.6 0.0 copy-start.17
  29.7 0.1 pad_add_fusion.where_ref
  29.7 0.7 turn.1.own_bias_ref.bias_ref
  30.5 0.0 copy-start.19
  30.5 2.0 %collective-permute-start = (f32[2,128,512]{2,1,0:T(8,128)S(1)}, f32[2,128,512]{2,1,0:T(8,128)S(1)}, u32[]{:S(2)}, u32[]{:S(2)}) collective-permute-start(f32[2,128,512]{2,1,0:T(8,128)S(1)} %turn.1.own_bias_ref.bias_ref), channel_id=1, source_target_pairs={{0,32},{32,64},{64,96},{96,0},{1,33},{33,65},{65,97},{97,1},{2,34}... | collective-permute-start | bytes 1572872 | tf_op jit(solution)/shard_map/ppermute | solution.py:382
  32.5 2.2 %collective-permute-start.1 = (f32[2,128,512]{2,1,0:T(8,128)S(1)}, f32[2,128,512]{2,1,0:T(8,128)S(1)}, u32[]{:S(2)}, u32[]{:S(2)}) collective-permute-start(f32[2,128,512]{2,1,0:T(8,128)S(1)} %turn.1.own_bias_ref.bias_ref), channel_id=1, source_target_pairs={{0,96},{32,0},{64,32},{96,64},{1,97},{33,1},{65,33},{97,65},{2,98}... | collective-permute-start | bytes 1572872 | tf_op jit(solution)/shard_map/ppermute | solution.py:382
  34.7 0.9 weights.1
  35.6 0.6 copy-done.6
  36.3 10.2 %collective-permute-done.refs_1_ = f32[2,128,512]{2,1,0:T(8,128)S(1)} collective-permute-done((f32[2,128,512]{2,1,0:T(8,128)S(1)}, f32[2,128,512]{2,1,0:T(8,128)S(1)}, u32[]{:S(2)}, u32[]{:S(2)}) %collective-permute-start) | collective-permute-done | bytes 524320 | tf_op jit(solution)/shard_map/ppermute | solution.py:382
  46.5 0.1 broadcast_in_dim.8.refs_4_.live_ref
  46.6 0.0 copy-start
  46.6 0.1 collective-permute-start.2
  46.7 3.3 %collective-permute-start.3 = (f32[2,128,512]{2,1,0:T(8,128)S(1)}, f32[2,128,512]{2,1,0:T(8,128)}, u32[]{:S(2)}, u32[]{:S(2)}) collective-permute-start(f32[2,128,512]{2,1,0:T(8,128)S(1)} %turn.1.own_bias_ref.bias_ref), channel_id=1, source_target_pairs={{0,64},{32,96},{64,0},{96,32},{1,65},{33,97},{65,1},{97,33},{2,66}... | collective-permute-start | bytes 1572872 | tf_op jit(solution)/shard_map/ppermute | solution.py:382
  50.1 1.0 copy-done.20
  51.1 13.6 %first.1 = (bf16[8,512,128]{2,1,0:T(8,128)(2,1)}, bf16[8,512,128]{2,1,0:T(8,128)(2,1)}, bf16[8,512,128]{2,1,0:T(8,128)(2,1)}, f32[8,512,128]{2,1,0:T(8,128)}, f3...) custom-call(s32[3]{0:T(128)} %copy-done.8, ...), custom_call_target="tpu_custom_call" | custom-call | flops 22000001024 | bytes 40000000 | tf_op jit(solution)/shard_map/first/pallas_call | solution.py:483
  64.7 1.1 collective-permute-start.6
  65.8 2.2 %collective-permute-start.7 = (s16[2,128,640]{2,1,0:T(8,128)(2,1)}, s16[2,128,640]{2,1,0:T(8,128)(2,1)S(1)}, u32[]{:S(2)}, u32[]{:S(2)}) collective-permute-start(s16[2,128,640]{2,1,0:T(8,128)(2,1)} %get-tuple-element.53), channel_id=1, source_target_pairs={{0,96},{32,0},{64,32},{96,64},{1,97},{33,1},{65,33},{97,65},{2,98}... | collective-permute-start | bytes 983048 | tf_op jit(solution)/shard_map/ppermute | solution.py:382
  68.0 0.0 collective-permute-done.3.far_bias_ref
  68.0 10.6 %middle.1 = (f32[8,192,128]{2,1,0:T(8,128)}, bf16[8,192,128]{2,1,0:T(8,128)(2,1)}, f32[8,128,512]{2,1,0:T(8,128)}, s16[2,64,640]{2,1,0:T(8,128)(2,1)}, s16[2,64,...) custom-call(s32[3]{0:T(128)} %copy-done.8, bf16[8,512,128]{2,1,0:T(8,128)(2,1)} %get-tuple-element.35.qd_ref, ...), custom_call_target="tpu_custom_call" | custom-call | flops 110000000 | bytes 200000 | tf_op jit(solution)/shard_map/middle/pallas_call | solution.py:502
  78.6 1.4 %collective-permute-start.4 = (s16[2,64,640]{2,1,0:T(8,128)(2,1)}, s16[2,64,640]{2,1,0:T(8,128)(2,1)S(1)}, u32[]{:S(2)}, u32[]{:S(2)}) collective-permute-start(s16[2,64,640]{2,1,0:T(8,128)(2,1)} %get-tuple-element.49), channel_id=1, source_target_pairs={{0,64},{32,96},{64,0},{96,32},{1,65},{33,97},{65,1},{97,33},{2,66}... | collective-permute-start | bytes 491528 | tf_op jit(solution)/shard_map/ppermute | solution.py:382
  80.0 2.4 %collective-permute-start.5 = (s16[2,64,640]{2,1,0:T(8,128)(2,1)}, s16[2,64,640]{2,1,0:T(8,128)(2,1)S(1)}, u32[]{:S(2)}, u32[]{:S(2)}) collective-permute-start(s16[2,64,640]{2,1,0:T(8,128)(2,1)} %get-tuple-element.50), channel_id=1, source_target_pairs={{0,80},{16,64},{32,112},{48,96},{64,16},{80,0},{96,48},{112,32},{1... | collective-permute-start | bytes 491528 | tf_op jit(solution)/shard_map/ppermute | solution.py:511
  82.4 0.0 collective-permute-done.7.refs_1_
  82.4 0.9 copy-done.5
  83.4 0.3 far.1
  83.6 3.0 %collective-permute-start.8 = (s16[2,64,640]{2,1,0:T(8,128)(2,1)S(1)}, s16[2,64,640]{2,1,0:T(8,128)(2,1)S(1)}, u32[]{:S(2)}, u32[]{:S(2)}) collective-permute-start(s16[2,64,640]{2,1,0:T(8,128)(2,1)S(1)} %far.1), channel_id=1, source_target_pairs={{0,16},{16,0},{1,17},{17,1},{2,18},{18,2},{3,19},{19,3},{4,20},{20... | collective-permute-start | bytes 491528 | tf_op jit(solution)/shard_map/ppermute | solution.py:382
  86.6 9.2 %last.1 = (f32[8,8,32,128]{3,2,1,0:T(8,128)}, f32[8,8,32,128]{3,2,1,0:T(8,128)}, bf16[8,8,32,128]{3,2,1,0:T(8,128)(2,1)}, bf16[8,8,32,128]{3,2,1,0:T(8,128)(2,1)}, f32[2,64,512]{2,1,0:T(8,128)}) custom-call(s32[3]{0:T(128)} %copy-done.8, bf16[8,512,128]{2,1,0:T(8,128)(2,1)} %get-tuple-element.35.qd_ref, bf16[8,512,128]{2,1,0:T(8,128)(2,1)} %get-tuple-element.36.kv_ref, ...), custom_call_target="tpu_custom_call" | custom-call | flops 110000000 | bytes 200000 | tf_op jit(solution)/shard_map/last/pallas_call | solution.py:518
  95.9 0.0 collective-permute-done.4.refs_2_
  95.9 0.0 copy-start.12
  95.9 0.1 collective-permute-start.9
  96.0 0.5 collective-permute-start.10
  96.5 0.9 copy-done.15
  97.5 1.1 lines.1
  98.6 0.2 collective-permute-start.11
  98.8 1.3 collective-permute-done.11.came_lines_ref
  100.0 1.6 %merge.1 = s16[8,9,32,256]{3,2,1,0:T(8,128)(2,1)S(1)} custom-call(s32[3]{0:T(128)S(1)} %copy-done.9, f32[8,8,32,128]{3,2,1,0:T(8,128)S(1)} %copy-done.12, f32[8,8,32,128]{3,2,1,0:T(8,128)S(1)} %collective-permute-done.9.came_dn_ref, bf16[8,8,32,128]{3,2,1,0:T(8,128)(2,1)S(1)} %copy-done.14, bf16[8,8,32,128]{3,2,1,0:T(8,128)(2,1)S(1)} %collective-permute-done.10.came_mix_ref, ...), custom_call_target="tpu_custom_call" | custom-call | flops 2200000000 | bytes 4000000 | tf_op jit(solution)/shard_map/merge/pallas_call | solution.py:546
  101.7 0.0 copy-start.11
  101.7 22.2 %all_to_all.16.came_ref.scales_ref.lines_ref = s16[8,9,32,256]{3,2,1,0:T(8,128)(2,1)S(1)} all-to-all(s16[8,9,32,256]{3,2,1,0:T(8,128)(2,1)S(1)} %merge.1), channel_id=1, replica_groups=mesh['z'=4,'yh'=2,'x'=4,'yl'=2,'c'=2] {'x','yl'}, dimensions={0} | all-to-all | bytes 2359296 | tf_op jit(solution)/shard_map/all_to_all | solution.py:550
  123.9 2.8 %finish.1 = (f32[64,32,128]{2,1,0:T(8,128)}, f32[64,32,128]{2,1,0:T(8,128)}) custom-call(f32[64,32,128]{2,1,0:T(8,128)S(1)} %copy-done.11, s16[8,9,32,256]{3,2,1,0:T(8,128)(2,1)S(1)} %all_to_all.16.came_ref.scales_ref.lines_ref, s16[8,9,32,256]{3,2,1,0:T(8,128)(2,1)S(1)} %all_to_all.16.came_ref.scales_ref.lines_ref, ...), custom_call_target="tpu_custom_call" | custom-call | flops 3300000000 | bytes 6000000 | tf_op jit(solution)/shard_map/finish/pallas_call | solution.py:555
  (41 shorter events, 0.1 us)
Async XLA Ops:
  2.3 1.2 copy-start.10
  3.5 1.0 copy-start.13
  26.1 20.4 %all-to-all-start.1 = ((bf16[8,8,32,256]{3,2,1,0:T(8,128)(2,1)}), bf16[8,8,32,256]{3,2,1,0:T(8,128)(2,1)S(1)}, u32[]{:S(2)}, u32[]{:S(2)}) async-start(bf16[8,8,32,256]{3,2,1,0:T(8,128)(2,1)} %after.1), calls=%async_computation.1 | async-start | bytes 2097152 | tf_op jit(solution)/shard_map/all_to_all | solution.py:459
  29.6 5.1 %copy-start.16 = (bf16[4,128,128]{2,1,0:T(8,128)(2,1)S(1)}, bf16[4,128,128]{2,1,0:T(8,128)(2,1)}, u32[]{:S(2)}) copy-start(bf16[4,128,128]{2,1,0:T(8,128)(2,1)} %w_proj_ref.1) | copy-start | bytes 393220
  29.6 5.1 %copy-start.17 = (bf16[128,128]{1,0:T(8,128)(2,1)S(1)}, bf16[128,128]{1,0:T(8,128)(2,1)}, u32[]{:S(2)}) copy-start(bf16[128,128]{1,0:T(8,128)(2,1)} %w_out_ref.3) | copy-start | bytes 98308
  29.7 5.9 %copy-start.8 = (s32[3]{0:T(128)}, s32[3]{0:T(128)S(1)}, u32[]{:S(2)}) copy-start(s32[3]{0:T(128)S(1)} %pad_add_fusion.where_ref) | copy-start | bytes 40
  30.5 16.2 %copy-start.1 = (f32[2,128,512]{2,1,0:T(8,128)}, f32[2,128,512]{2,1,0:T(8,128)S(1)}, u32[]{:S(2)}) copy-start(f32[2,128,512]{2,1,0:T(8,128)S(1)} %turn.1.own_bias_ref.bias_ref) | copy-start | bytes 1572868
  30.5 16.0 %copy-start.19 = (s32[512]{0:T(512)S(1)}, s32[512]{0:T(512)}, u32[]{:S(2)}) copy-start(s32[512]{0:T(512)} %param.7) | copy-start | bytes 6148
  30.5 15.9 %collective-permute-start = (f32[2,128,512]{2,1,0:T(8,128)S(1)}, f32[2,128,512]{2,1,0:T(8,128)S(1)}, u32[]{:S(2)}, u32[]{:S(2)}) collective-permute-start(f32[2,128,512]{2,1,0:T(8,128)S(1)} %turn.1.own_bias_ref.bias_ref), channel_id=1, source_target_pairs={{0,32},{32,64},{64,96},{96,0},{1,33},{33,65},{65,97},{97,1},{2,34}... | collective-permute-start | bytes 1572872 | tf_op jit(solution)/shard_map/ppermute | solution.py:382
  32.5 14.0 %collective-permute-start.1 = (f32[2,128,512]{2,1,0:T(8,128)S(1)}, f32[2,128,512]{2,1,0:T(8,128)S(1)}, u32[]{:S(2)}, u32[]{:S(2)}) collective-permute-start(f32[2,128,512]{2,1,0:T(8,128)S(1)} %turn.1.own_bias_ref.bias_ref), channel_id=1, source_target_pairs={{0,96},{32,0},{64,32},{96,64},{1,97},{33,1},{65,33},{97,65},{2,98}... | collective-permute-start | bytes 1572872 | tf_op jit(solution)/shard_map/ppermute | solution.py:382
  35.6 0.6 copy-start.6
  36.3 14.8 %copy-start.7 = (bf16[128,256]{1,0:T(8,128)(2,1)}, bf16[128,256]{1,0:T(8,128)(2,1)S(1)}, u32[]{:S(2)}) copy-start(bf16[128,256]{1,0:T(8,128)(2,1)S(1)} %get-tuple-element.33.refs_3_.w_in_ref) | copy-start | bytes 196612
  36.3 14.8 %copy-start.18 = (bf16[128,128]{1,0:T(8,128)(2,1)}, bf16[128,128]{1,0:T(8,128)(2,1)S(1)}, u32[]{:S(2)}) copy-start(bf16[128,128]{1,0:T(8,128)(2,1)S(1)} %get-tuple-element.34.w_dm_ref) | copy-start | bytes 98308
  46.5 4.6 %copy-start.3 = (f32[2,128,512]{2,1,0:T(8,128)}, f32[2,128,512]{2,1,0:T(8,128)S(1)}, u32[]{:S(2)}) copy-start(f32[2,128,512]{2,1,0:T(8,128)S(1)} %collective-permute-done.refs_1_) | copy-start | bytes 1572868
  46.5 4.6 %copy-start.4 = (f32[2,128,512]{2,1,0:T(8,128)}, f32[2,128,512]{2,1,0:T(8,128)S(1)}, u32[]{:S(2)}) copy-start(f32[2,128,512]{2,1,0:T(8,128)S(1)} %collective-permute-done.1.refs_2_.refs_0_) | copy-start | bytes 1572868
  46.6 4.4 %copy-start.2 = (s32[512,128]{1,0:T(8,128)}, s32[512,128]{1,0:T(8,128)S(1)}, u32[]{:S(2)}) copy-start(s32[512,128]{1,0:T(8,128)S(1)} %broadcast_in_dim.8.refs_4_.live_ref) | copy-start | bytes 786436
  46.6 4.4 %copy-start = (bf16[8,8,32,256]{3,2,1,0:T(8,128)(2,1)}, bf16[8,8,32,256]{3,2,1,0:T(8,128)(2,1)S(1)}, u32[]{:S(2)}) copy-start(bf16[8,8,32,256]{3,2,1,0:T(8,128)(2,1)S(1)} %after_own.1.own_ref) | copy-start | bytes 3145732
  46.6 3.4 %collective-permute-start.2 = (bf16[8,8,32,256]{3,2,1,0:T(8,128)(2,1)S(1)}, bf16[8,8,32,256]{3,2,1,0:T(8,128)(2,1)S(1)}, u32[]{:S(2)}, u32[]{:S(2)}) collective-permute-start(bf16[8,8,32,256]{3,2,1,0:T(8,128)(2,1)S(1)} %after_own.1.own_ref), channel_id=1, source_target_pairs={{0,1},{1,0},{2,3},{3,2},{4,5},{5,4},{6,7},{7,6},{8,9},{9,8},{10,11... | collective-permute-start | bytes 3145736 | tf_op jit(solution)/shard_map/ppermute | solution.py:382
  46.7 21.2 %collective-permute-start.3 = (f32[2,128,512]{2,1,0:T(8,128)S(1)}, f32[2,128,512]{2,1,0:T(8,128)}, u32[]{:S(2)}, u32[]{:S(2)}) collective-permute-start(f32[2,128,512]{2,1,0:T(8,128)S(1)} %turn.1.own_bias_ref.bias_ref), channel_id=1, source_target_pairs={{0,64},{32,96},{64,0},{96,32},{1,65},{33,97},{65,1},{97,33},{2,66}... | collective-permute-start | bytes 1572872 | tf_op jit(solution)/shard_map/ppermute | solution.py:382
  50.1 1.0 copy-start.20
  64.7 17.8 %collective-permute-start.6 = (s16[2,128,640]{2,1,0:T(8,128)(2,1)}, s16[2,128,640]{2,1,0:T(8,128)(2,1)S(1)}, u32[]{:S(2)}, u32[]{:S(2)}) collective-permute-start(s16[2,128,640]{2,1,0:T(8,128)(2,1)} %get-tuple-element.52), channel_id=1, source_target_pairs={{0,32},{32,64},{64,96},{96,0},{1,33},{33,65},{65,97},{97,1},{2,34}... | collective-permute-start | bytes 983048 | tf_op jit(solution)/shard_map/ppermute | solution.py:382
  65.8 16.7 %collective-permute-start.7 = (s16[2,128,640]{2,1,0:T(8,128)(2,1)}, s16[2,128,640]{2,1,0:T(8,128)(2,1)S(1)}, u32[]{:S(2)}, u32[]{:S(2)}) collective-permute-start(s16[2,128,640]{2,1,0:T(8,128)(2,1)} %get-tuple-element.53), channel_id=1, source_target_pairs={{0,96},{32,0},{64,32},{96,64},{1,97},{33,1},{65,33},{97,65},{2,98}... | collective-permute-start | bytes 983048 | tf_op jit(solution)/shard_map/ppermute | solution.py:382
  78.6 17.3 %collective-permute-start.4 = (s16[2,64,640]{2,1,0:T(8,128)(2,1)}, s16[2,64,640]{2,1,0:T(8,128)(2,1)S(1)}, u32[]{:S(2)}, u32[]{:S(2)}) collective-permute-start(s16[2,64,640]{2,1,0:T(8,128)(2,1)} %get-tuple-element.49), channel_id=1, source_target_pairs={{0,64},{32,96},{64,0},{96,32},{1,65},{33,97},{65,1},{97,33},{2,66}... | collective-permute-start | bytes 491528 | tf_op jit(solution)/shard_map/ppermute | solution.py:382
  80.0 15.9 %collective-permute-start.5 = (s16[2,64,640]{2,1,0:T(8,128)(2,1)}, s16[2,64,640]{2,1,0:T(8,128)(2,1)S(1)}, u32[]{:S(2)}, u32[]{:S(2)}) collective-permute-start(s16[2,64,640]{2,1,0:T(8,128)(2,1)} %get-tuple-element.50), channel_id=1, source_target_pairs={{0,80},{16,64},{32,112},{48,96},{64,16},{80,0},{96,48},{112,32},{1... | collective-permute-start | bytes 491528 | tf_op jit(solution)/shard_map/ppermute | solution.py:511
  82.4 1.0 copy-start.5
  83.6 12.3 %collective-permute-start.8 = (s16[2,64,640]{2,1,0:T(8,128)(2,1)S(1)}, s16[2,64,640]{2,1,0:T(8,128)(2,1)S(1)}, u32[]{:S(2)}, u32[]{:S(2)}) collective-permute-start(s16[2,64,640]{2,1,0:T(8,128)(2,1)S(1)} %far.1), channel_id=1, source_target_pairs={{0,16},{16,0},{1,17},{17,1},{2,18},{18,2},{3,19},{19,3},{4,20},{20... | collective-permute-start | bytes 491528 | tf_op jit(solution)/shard_map/ppermute | solution.py:382
  86.6 9.9 %copy-start.9 = (s32[3]{0:T(128)S(1)}, s32[3]{0:T(128)}, u32[]{:S(2)}) copy-start(s32[3]{0:T(128)} %copy-done.8) | copy-start | bytes 40
  95.9 4.1 %copy-start.12 = (f32[8,8,32,128]{3,2,1,0:T(8,128)S(1)}, f32[8,8,32,128]{3,2,1,0:T(8,128)}, u32[]{:S(2)}) copy-start(f32[8,8,32,128]{3,2,1,0:T(8,128)} %get-tuple-element.46.keep_dn_ref) | copy-start | bytes 3145732
  95.9 4.1 %copy-start.14 = (bf16[8,8,32,128]{3,2,1,0:T(8,128)(2,1)S(1)}, bf16[8,8,32,128]{3,2,1,0:T(8,128)(2,1)}, u32[]{:S(2)}) copy-start(bf16[8,8,32,128]{3,2,1,0:T(8,128)(2,1)} %get-tuple-element.55.keep_mix_ref) | copy-start | bytes 1572868
  95.9 4.1 %collective-permute-start.9 = (f32[8,8,32,128]{3,2,1,0:T(8,128)}, f32[8,8,32,128]{3,2,1,0:T(8,128)S(1)}, u32[]{:S(2)}, u32[]{:S(2)}) collective-permute-start(f32[8,8,32,128]{3,2,1,0:T(8,128)} %get-tuple-element.54), channel_id=1, source_target_pairs={{0,1},{1,0},{2,3},{3,2},{4,5},{5,4},{6,7},{7,6},{8,9},{9,8},{10,11... | collective-permute-start | bytes 3145736 | tf_op jit(solution)/shard_map/ppermute | solution.py:382
  96.0 4.0 %collective-permute-start.10 = (bf16[8,8,32,128]{3,2,1,0:T(8,128)(2,1)}, bf16[8,8,32,128]{3,2,1,0:T(8,128)(2,1)S(1)}, u32[]{:S(2)}, u32[]{:S(2)}) collective-permute-start(bf16[8,8,32,128]{3,2,1,0:T(8,128)(2,1)} %get-tuple-element.56), channel_id=1, source_target_pairs={{0,1},{1,0},{2,3},{3,2},{4,5},{5,4},{6,7},{7,6},{8,9},{9,8},{10,11... | collective-permute-start | bytes 1572872 | tf_op jit(solution)/shard_map/ppermute | solution.py:382
  96.5 1.0 copy-start.15
  98.6 1.4 %collective-permute-start.11 = (s16[8,32,256]{2,1,0:T(8,128)(2,1)S(1)}, s16[8,32,256]{2,1,0:T(8,128)(2,1)S(1)}, u32[]{:S(2)}, u32[]{:S(2)}) collective-permute-start(s16[8,32,256]{2,1,0:T(8,128)(2,1)S(1)} %get-tuple-element.59), channel_id=1, source_target_pairs={{0,1},{1,0},{2,3},{3,2},{4,5},{5,4},{6,7},{7,6},{8,9},{9,8},{10,11... | collective-permute-start | bytes 393224 | tf_op jit(solution)/shard_map/ppermute | solution.py:382
  101.7 22.2 %copy-start.11 = (f32[64,32,128]{2,1,0:T(8,128)S(1)}, f32[64,32,128]{2,1,0:T(8,128)}, u32[]{:S(2)}) copy-start(f32[64,32,128]{2,1,0:T(8,128)} %pair_ref.3) | copy-start | bytes 3145732
